TPU v7x, 32 devices: a whole 2x2x4 slice. The times are simulated.
32 devices in a mesh: src: 4 (over x, core), tile: 8 (over z, y).
Axes of the slice: x: 2, y: 2, z: 4, core: 2. Of those that a mesh axis runs over, the one named last changes fastest.
Arguments:
- mask_logits: float32 [4096, 512], P('tile'), may hold values from -10 to 10
- target: int32 [4096, 512], P('tile'), may hold values 0 or 1
- weights: float32 [64], P('src'), may hold values from 0.0078125 to 0.03125
- shifts: int32 [64, 2], P('src'), may hold values from -11 to 11
Outputs:
- mask_grad: float32 [4096, 512], P('tile')
- weight_grad: float32 [64], P('src')
- loss: float32 [], replicated
All inputs are finite; a program needn't handle non-finite values. No bound on the sum of `target` on one device may be relied on, other than what follows from the above.
Results may differ from a plain program's by a relative error of at most 0.0008.
The roundings to bfloat16 on the way count: a program that leaves them out, or rounds other values in their place, can miss the bound.
Values may be sent and summed in bfloat16 or wider, within the bound.
A program may use at most 64 MiB of HBM per device.

v0:
```python
import jax
import jax.numpy as jnp
from jax import lax
from jax.sharding import PartitionSpec as P

FREQS = 64
RADIUS = 20
MARGIN = 64


STEEPNESS = 12.0
THRESHOLD = 0.2
HIGHEST = lax.Precision.HIGHEST


def extended(x, sides, width):
    for axis, dim in sides:
        peers, length = (lax.axis_size(axis), x.shape[dim])
        up = [(i, (i + 1) % peers) for i in range(peers - 1)]
        down = [(j, i) for i, j in up]
        last = lax.slice_in_dim(x, length - width, length, axis=dim)
        first = lax.slice_in_dim(x, 0, width, axis=dim)
        before = lax.ppermute(last, axis, up)
        after = lax.ppermute(first, axis, down)
        x = jnp.concatenate([before, x, after], axis=dim)
    return x


def angles(length_used, offset, period):
    position = jnp.arange(length_used, dtype=jnp.int32)[:, None] + offset
    frequency = jnp.arange(FREQS, dtype=jnp.int32)[None, :] - FREQS // 2
    cycles = jnp.mod(position * frequency, period).astype(jnp.float32)
    angle_value = cycles * jnp.float32(2.0 * 3.141592653589793 / period)
    return (jnp.cos(angle_value), jnp.sin(angle_value))


def make_tables(tile_rows, frame_rows, col_count):
    column_cosine, column_sine = angles(col_count, 0, col_count)
    column_forward = jnp.concatenate([column_cosine, -column_sine], 1).astype(jnp.bfloat16)
    frame_cosine, frame_sine = angles(frame_rows, 0, frame_rows)
    row_forward = jnp.concatenate([frame_cosine.T, -frame_sine.T], 0).astype(jnp.bfloat16)
    owned_cosine, owned_sine = angles(tile_rows, MARGIN, frame_rows)
    row_inverse = (jnp.concatenate([owned_cosine, owned_sine], 1) / frame_rows).astype(jnp.bfloat16)
    cosine_scaled = column_cosine.T / col_count
    sine_scaled = column_sine.T / col_count
    upper_block = jnp.concatenate([cosine_scaled, sine_scaled], 1)
    lower_block = jnp.concatenate([-sine_scaled, cosine_scaled], 1)
    column_inverse = jnp.concatenate([upper_block, lower_block], 0).astype(jnp.bfloat16)
    return (column_forward, row_forward, row_inverse, column_inverse)


def pupil_masks(shifts):
    frequency = jnp.arange(FREQS, dtype=jnp.int32) - FREQS // 2
    offset_across = frequency[None, :, None] - shifts[:, 0][:, None, None]
    offset_along = frequency[None, None, :] - shifts[:, 1][:, None, None]
    inside = offset_across * offset_across + offset_along * offset_along <= RADIUS * RADIUS
    return inside.astype(jnp.float32)


def spectrum(framed, column_forward, row_forward):
    column_part = jnp.dot(framed, column_forward, preferred_element_type=jnp.float32).astype(
        jnp.bfloat16
    )
    product = jnp.dot(row_forward, column_part, preferred_element_type=jnp.float32)
    spectrum_real = (product[:FREQS, :FREQS] - product[FREQS:, FREQS:]).astype(jnp.bfloat16)
    spectrum_imag = (product[:FREQS, FREQS:] + product[FREQS:, :FREQS]).astype(jnp.bfloat16)
    return (spectrum_real, spectrum_imag)


def pupil_blocks(pupils, spectrum_real, spectrum_imag):
    pass_real = pupils * spectrum_real.astype(jnp.float32)
    pass_imag = pupils * spectrum_imag.astype(jnp.float32)
    upper_block = jnp.concatenate([pass_real, pass_imag], 2)
    lower_block = jnp.concatenate([-pass_imag, pass_real], 2)
    return jnp.concatenate([upper_block, lower_block], 1).astype(jnp.bfloat16)


def images(blocks, row_inverse, column_inverse):
    row_field = jnp.einsum(
        "pk,skj->spj", row_inverse, blocks, preferred_element_type=jnp.float32
    ).astype(jnp.bfloat16)
    source_count, tile_rows, doubled_freqs = row_field.shape
    fields = jnp.dot(
        row_field.reshape(source_count * tile_rows, doubled_freqs),
        column_inverse,
        preferred_element_type=jnp.float32,
    )
    return fields.reshape(source_count, tile_rows, -1)


def field_powers(fields):
    col_count = fields.shape[2] // 2
    return (
        fields[:, :, :col_count] * fields[:, :, :col_count]
        + fields[:, :, col_count:] * fields[:, :, col_count:]
    )


def apply_resist(intensity, target_rows):
    printed = jax.nn.sigmoid(STEEPNESS * (intensity - THRESHOLD))
    error_value = printed - target_rows.astype(jnp.float32)
    cotangent = 2.0 * STEEPNESS * error_value * printed * (1.0 - printed)
    return (cotangent, jnp.sum(error_value * error_value))


def frame_gradient(grad_real, grad_imag, column_forward, row_forward):
    upper_block = jnp.concatenate([grad_real, grad_imag], 1)
    lower_block = jnp.concatenate([grad_imag, -grad_real], 1)
    product_grad = jnp.concatenate([upper_block, lower_block], 0)
    column_grad = jnp.dot(row_forward.astype(jnp.float32).T, product_grad, precision=HIGHEST)
    return jnp.dot(column_grad, column_forward.astype(jnp.float32).T, precision=HIGHEST)


def on_device(mask_logits, target, weights, shifts):
    tile_rows, col_count = mask_logits.shape
    frame_rows = tile_rows + 2 * MARGIN
    column_forward, row_forward, row_inverse, column_inverse = make_tables(
        tile_rows, frame_rows, col_count
    )
    opening = jax.nn.sigmoid(mask_logits)
    framed = extended(opening.astype(jnp.bfloat16), (("tile", 0),), MARGIN)
    spectrum_real, spectrum_imag = spectrum(framed, column_forward, row_forward)
    pupils = pupil_masks(shifts)
    source_count = weights.shape[0]
    pupil_pairs = pupils.reshape(source_count // 2, 2, FREQS, FREQS)
    weight_pairs = weights.reshape(source_count // 2, 2)

    def forward_step(running, pair_item):
        pupil_pair, weight_pair = pair_item
        fields = images(
            pupil_blocks(pupil_pair, spectrum_real, spectrum_imag), row_inverse, column_inverse
        )
        return (running + jnp.sum(weight_pair[:, None, None] * field_powers(fields), 0), None)

    partial_image, unused = lax.scan(
        forward_step, jnp.zeros((tile_rows, col_count), jnp.float32), (pupil_pairs, weight_pairs)
    )
    intensity = lax.psum(partial_image, "src")
    cotangent, error_sum = apply_resist(intensity, target)
    doubled = jnp.concatenate([cotangent, cotangent], 1)

    def backward_step(running, pair_item):
        pupil_pair, weight_pair = pair_item
        fields = images(
            pupil_blocks(pupil_pair, spectrum_real, spectrum_imag), row_inverse, column_inverse
        )
        source_terms = jnp.sum(cotangent[None] * field_powers(fields), axis=(1, 2))
        scaling = (2.0 * weight_pair)[:, None, None] * doubled[None]
        field_grad = (scaling * fields).astype(jnp.bfloat16)
        row_grad = lax.dot_general(
            field_grad.reshape(-1, 2 * col_count),
            column_inverse,
            (((1,), (1,)), ((), ())),
            preferred_element_type=jnp.float32,
        )
        row_grad = row_grad.astype(jnp.bfloat16).reshape(2, tile_rows, -1)
        block_grad = jnp.einsum(
            "pk,spj->skj", row_inverse, row_grad, preferred_element_type=jnp.float32
        )
        grad_real = jnp.sum(
            pupil_pair * (block_grad[:, :FREQS, :FREQS] + block_grad[:, FREQS:, FREQS:]), 0
        )
        grad_imag = jnp.sum(
            pupil_pair * (block_grad[:, :FREQS, FREQS:] - block_grad[:, FREQS:, :FREQS]), 0
        )
        return ((running[0] + grad_real, running[1] + grad_imag), source_terms)

    zero_spectrum = jnp.zeros((FREQS, FREQS), jnp.float32)
    grads, pair_terms = lax.scan(
        backward_step, (zero_spectrum, zero_spectrum), (pupil_pairs, weight_pairs)
    )
    source_terms = pair_terms.reshape(source_count)
    grad_real, grad_imag = lax.psum((grads[0], grads[1]), "src")
    frame_grad = frame_gradient(grad_real, grad_imag, column_forward, row_forward)
    margin_grads = jnp.concatenate([frame_grad[:MARGIN], frame_grad[MARGIN + tile_rows :]], 0)
    beside_all = extended(margin_grads.astype(jnp.bfloat16), (("tile", 0),), MARGIN).astype(
        margin_grads.dtype
    )
    owned_grads = frame_grad[MARGIN : MARGIN + tile_rows]
    owned_grads = owned_grads.at[:MARGIN].add(beside_all[:MARGIN])
    owned_grads = owned_grads.at[tile_rows - MARGIN :].add(beside_all[3 * MARGIN :])
    mask_grad = owned_grads * opening * (1.0 - opening)
    pixel_total = tile_rows * col_count * lax.axis_size("tile")
    weight_sum, error_total = lax.psum((source_terms, error_sum), "tile")
    return (mask_grad, weight_sum / pixel_total, error_total / pixel_total)


def solution(mesh):
    placed = (P("tile", None), P("tile", None), P("src"), P("src", None))
    return jax.shard_map(
        on_device,
        mesh=mesh,
        in_specs=placed,
        out_specs=(P("tile", None), P("src"), P()),
        check_vma=False,
    )
```

profile of v0, /device:TPU:0, one launch (start us, length us, event | category | flops | bytes accessed | tf_op | source)
XLA Modules:
  0.0 275.1 jit_solution(18156360879937922217)
XLA Ops:
  7.2 1.5 fusion.70
  8.8 4.9 %collective-permute-start = (bf16[64,512]{1,0:T(8,128)(2,1)S(1)}, bf16[64,512]{1,0:T(8,128)(2,1)S(1)}, u32[]{:S(2)}, u32[]{:S(2)}) collective-permute-start(bf16[64,512]{1,0:T(8,128)(2,1)S(1)} %get-tuple-element.345), channel_id=1, source_target_pairs={{0,1},{1,2},{2,3},{3,4},{4,5},{5,6},{6,7},{8,9},{9,10},{10,11},{11... | collective-permute-start | bytes 196616 | tf_op jit(solution)/shard_map/ppermute | solution.py:23
  18.3 1.5 collective-permute-done.1
  20.6 50.5 %while.28 = (s32[]{:T(128)}, f32[512,512]{1,0:T(8,128)S(1)}, f32[8,2]{1,0:T(8,128)S(1)}, f32[8,2,64,64]{2,3,1,0:T(8,128)S(1)}, bf16[64,64]{0,1:T(8,128)(2,1)S(1)...) while((s32[]{:T(128)}, f32[512,512]{1,0:T(8,128)S(1)}, ...), condition=%wide.region_2.3_spmd.clone, body=%wide.region_0.2_spmd.clone.sunk | while | flops 305324032 | bytes 13189263 | solution.py:135
  20.7 2.9 %fusion.144 = f32[2,512,1024]{2,1,0:T(8,128)} fusion(bf16[128,1024]{1,0:T(8,128)(2,1)S(1)} %get-tuple-element.535, bf16[512,128]{1,0:T(8,128)(2,1)S(1)} %get-tuple-element.534, bf16[2,64,64]{1,2,0:T(8,128)(2,1)S(1)} %get-tuple-element.484, bf16[2,64,64]{1,2,0:T(8,128)(2,1)S(1)} %get-tuple-element.485, bf16[2,64,64]{1,2,0:T(8,128)(2,1)S(1)} %get-tuple-element.486), kind=kOutput, calls=%fused_computation.7.clone.1 | convolution fusion | flops 302383104 | bytes 4636672 | tf_op jit(solution)/shard_map/while/body/eval_jaxpr/dot_general | solution.py:83
  23.6 2.9 %fusion.145 = f32[512,512]{1,0:T(8,128)S(1)} fusion(f32[2,512,1024]{2,1,0:T(8,128)} %fusion.144, f32[2]{0:T(128)S(1)} %dynamic-slice_bitcast_fusion.2), kind=kLoop, calls=%fused_computation.3.clone.1 | loop fusion | flops 2359296 | bytes 5242888 | tf_op jit(solution)/shard_map/while/body/eval_jaxpr/reduce_sum | solution.py:133
  27.0 2.9 %fusion.144 = f32[2,512,1024]{2,1,0:T(8,128)} fusion(bf16[128,1024]{1,0:T(8,128)(2,1)S(1)} %get-tuple-element.535, bf16[512,128]{1,0:T(8,128)(2,1)S(1)} %get-tuple-element.534, bf16[2,64,64]{1,2,0:T(8,128)(2,1)S(1)} %get-tuple-element.484, bf16[2,64,64]{1,2,0:T(8,128)(2,1)S(1)} %get-tuple-element.485, bf16[2,64,64]{1,2,0:T(8,128)(2,1)S(1)} %get-tuple-element.486), kind=kOutput, calls=%fused_computation.7.clone.1 | convolution fusion | flops 302383104 | bytes 4636672 | tf_op jit(solution)/shard_map/while/body/eval_jaxpr/dot_general | solution.py:83
  29.9 2.9 %fusion.145 = f32[512,512]{1,0:T(8,128)S(1)} fusion(f32[2,512,1024]{2,1,0:T(8,128)} %fusion.144, f32[2]{0:T(128)S(1)} %dynamic-slice_bitcast_fusion.2), kind=kLoop, calls=%fused_computation.3.clone.1 | loop fusion | flops 2359296 | bytes 5242888 | tf_op jit(solution)/shard_map/while/body/eval_jaxpr/reduce_sum | solution.py:133
  33.3 2.9 %fusion.144 = f32[2,512,1024]{2,1,0:T(8,128)} fusion(bf16[128,1024]{1,0:T(8,128)(2,1)S(1)} %get-tuple-element.535, bf16[512,128]{1,0:T(8,128)(2,1)S(1)} %get-tuple-element.534, bf16[2,64,64]{1,2,0:T(8,128)(2,1)S(1)} %get-tuple-element.484, bf16[2,64,64]{1,2,0:T(8,128)(2,1)S(1)} %get-tuple-element.485, bf16[2,64,64]{1,2,0:T(8,128)(2,1)S(1)} %get-tuple-element.486), kind=kOutput, calls=%fused_computation.7.clone.1 | convolution fusion | flops 302383104 | bytes 4636672 | tf_op jit(solution)/shard_map/while/body/eval_jaxpr/dot_general | solution.py:83
  36.2 2.9 %fusion.145 = f32[512,512]{1,0:T(8,128)S(1)} fusion(f32[2,512,1024]{2,1,0:T(8,128)} %fusion.144, f32[2]{0:T(128)S(1)} %dynamic-slice_bitcast_fusion.2), kind=kLoop, calls=%fused_computation.3.clone.1 | loop fusion | flops 2359296 | bytes 5242888 | tf_op jit(solution)/shard_map/while/body/eval_jaxpr/reduce_sum | solution.py:133
  39.6 2.9 %fusion.144 = f32[2,512,1024]{2,1,0:T(8,128)} fusion(bf16[128,1024]{1,0:T(8,128)(2,1)S(1)} %get-tuple-element.535, bf16[512,128]{1,0:T(8,128)(2,1)S(1)} %get-tuple-element.534, bf16[2,64,64]{1,2,0:T(8,128)(2,1)S(1)} %get-tuple-element.484, bf16[2,64,64]{1,2,0:T(8,128)(2,1)S(1)} %get-tuple-element.485, bf16[2,64,64]{1,2,0:T(8,128)(2,1)S(1)} %get-tuple-element.486), kind=kOutput, calls=%fused_computation.7.clone.1 | convolution fusion | flops 302383104 | bytes 4636672 | tf_op jit(solution)/shard_map/while/body/eval_jaxpr/dot_general | solution.py:83
  42.6 2.9 %fusion.145 = f32[512,512]{1,0:T(8,128)S(1)} fusion(f32[2,512,1024]{2,1,0:T(8,128)} %fusion.144, f32[2]{0:T(128)S(1)} %dynamic-slice_bitcast_fusion.2), kind=kLoop, calls=%fused_computation.3.clone.1 | loop fusion | flops 2359296 | bytes 5242888 | tf_op jit(solution)/shard_map/while/body/eval_jaxpr/reduce_sum | solution.py:133
  45.9 2.9 %fusion.144 = f32[2,512,1024]{2,1,0:T(8,128)} fusion(bf16[128,1024]{1,0:T(8,128)(2,1)S(1)} %get-tuple-element.535, bf16[512,128]{1,0:T(8,128)(2,1)S(1)} %get-tuple-element.534, bf16[2,64,64]{1,2,0:T(8,128)(2,1)S(1)} %get-tuple-element.484, bf16[2,64,64]{1,2,0:T(8,128)(2,1)S(1)} %get-tuple-element.485, bf16[2,64,64]{1,2,0:T(8,128)(2,1)S(1)} %get-tuple-element.486), kind=kOutput, calls=%fused_computation.7.clone.1 | convolution fusion | flops 302383104 | bytes 4636672 | tf_op jit(solution)/shard_map/while/body/eval_jaxpr/dot_general | solution.py:83
  48.9 2.9 %fusion.145 = f32[512,512]{1,0:T(8,128)S(1)} fusion(f32[2,512,1024]{2,1,0:T(8,128)} %fusion.144, f32[2]{0:T(128)S(1)} %dynamic-slice_bitcast_fusion.2), kind=kLoop, calls=%fused_computation.3.clone.1 | loop fusion | flops 2359296 | bytes 5242888 | tf_op jit(solution)/shard_map/while/body/eval_jaxpr/reduce_sum | solution.py:133
  52.2 2.9 %fusion.144 = f32[2,512,1024]{2,1,0:T(8,128)} fusion(bf16[128,1024]{1,0:T(8,128)(2,1)S(1)} %get-tuple-element.535, bf16[512,128]{1,0:T(8,128)(2,1)S(1)} %get-tuple-element.534, bf16[2,64,64]{1,2,0:T(8,128)(2,1)S(1)} %get-tuple-element.484, bf16[2,64,64]{1,2,0:T(8,128)(2,1)S(1)} %get-tuple-element.485, bf16[2,64,64]{1,2,0:T(8,128)(2,1)S(1)} %get-tuple-element.486), kind=kOutput, calls=%fused_computation.7.clone.1 | convolution fusion | flops 302383104 | bytes 4636672 | tf_op jit(solution)/shard_map/while/body/eval_jaxpr/dot_general | solution.py:83
  55.2 2.9 %fusion.145 = f32[512,512]{1,0:T(8,128)S(1)} fusion(f32[2,512,1024]{2,1,0:T(8,128)} %fusion.144, f32[2]{0:T(128)S(1)} %dynamic-slice_bitcast_fusion.2), kind=kLoop, calls=%fused_computation.3.clone.1 | loop fusion | flops 2359296 | bytes 5242888 | tf_op jit(solution)/shard_map/while/body/eval_jaxpr/reduce_sum | solution.py:133
  58.6 2.9 %fusion.144 = f32[2,512,1024]{2,1,0:T(8,128)} fusion(bf16[128,1024]{1,0:T(8,128)(2,1)S(1)} %get-tuple-element.535, bf16[512,128]{1,0:T(8,128)(2,1)S(1)} %get-tuple-element.534, bf16[2,64,64]{1,2,0:T(8,128)(2,1)S(1)} %get-tuple-element.484, bf16[2,64,64]{1,2,0:T(8,128)(2,1)S(1)} %get-tuple-element.485, bf16[2,64,64]{1,2,0:T(8,128)(2,1)S(1)} %get-tuple-element.486), kind=kOutput, calls=%fused_computation.7.clone.1 | convolution fusion | flops 302383104 | bytes 4636672 | tf_op jit(solution)/shard_map/while/body/eval_jaxpr/dot_general | solution.py:83
  61.5 2.9 %fusion.145 = f32[512,512]{1,0:T(8,128)S(1)} fusion(f32[2,512,1024]{2,1,0:T(8,128)} %fusion.144, f32[2]{0:T(128)S(1)} %dynamic-slice_bitcast_fusion.2), kind=kLoop, calls=%fused_computation.3.clone.1 | loop fusion | flops 2359296 | bytes 5242888 | tf_op jit(solution)/shard_map/while/body/eval_jaxpr/reduce_sum | solution.py:133
  64.9 2.9 %fusion.144 = f32[2,512,1024]{2,1,0:T(8,128)} fusion(bf16[128,1024]{1,0:T(8,128)(2,1)S(1)} %get-tuple-element.535, bf16[512,128]{1,0:T(8,128)(2,1)S(1)} %get-tuple-element.534, bf16[2,64,64]{1,2,0:T(8,128)(2,1)S(1)} %get-tuple-element.484, bf16[2,64,64]{1,2,0:T(8,128)(2,1)S(1)} %get-tuple-element.485, bf16[2,64,64]{1,2,0:T(8,128)(2,1)S(1)} %get-tuple-element.486), kind=kOutput, calls=%fused_computation.7.clone.1 | convolution fusion | flops 302383104 | bytes 4636672 | tf_op jit(solution)/shard_map/while/body/eval_jaxpr/dot_general | solution.py:83
  67.8 2.9 %fusion.145 = f32[512,512]{1,0:T(8,128)S(1)} fusion(f32[2,512,1024]{2,1,0:T(8,128)} %fusion.144, f32[2]{0:T(128)S(1)} %dynamic-slice_bitcast_fusion.2), kind=kLoop, calls=%fused_computation.3.clone.1 | loop fusion | flops 2359296 | bytes 5242888 | tf_op jit(solution)/shard_map/while/body/eval_jaxpr/reduce_sum | solution.py:133
  72.1 37.4 %all-reduce.4.cloned.1.call-done = f32[512,512]{1,0:T(8,128)} async-done(((f32[512,512]{1,0:T(8,128)}), f32[512,512]{1,0:T(8,128)}) %all-reduce.4.cloned.1.call-update) | async-done | bytes 1048592 | tf_op jit(solution)/shard_map/psum | solution.py:138
  109.5 2.6 multiply_reduce_fusion
  112.1 1.6 pad_maximum_fusion
  113.8 107.0 %while.29 = (s32[]{:T(128)}, f32[64,64]{0,1:T(8,128)}, f32[64,64]{0,1:T(8,128)}, f32[8,2]{1,0:T(8,128)}, f32[8,2,64,64]{2,3,1,0:T(8,128)S(1)}, /*index=5*/f32[8,...) while((s32[]{:T(128)}, f32[64,64]{0,1:T(8,128)}, ...), condition=%wide.region_8.9_spmd.clone, body=%wide.region_4.8_spmd.clone.sunk | while | flops 610385920 | bytes 19841912 | solution.py:169
  115.1 4.6 %multiply_convert_fusion.3 = (bf16[2,512,1024]{2,1,0:T(8,128)(2,1)S(1)}, f32[2,512,1024]{2,1,0:T(8,128)}) fusion(f32[512,1024]{1,0:T(8,128)} %get-tuple-element.572, f32[2]{0:T(128)} %multiply_bitcast_fusion.2, bf16[128,1024]{1,0:T(8,128)(2,1)S(1)} %get-tuple-element.576, bf16[512,128]{1,0:T(8,128)(2,1)S(1)} %get-tuple-element.575, ...), kind=kOutput, calls=%fused_computation.25.clone.1 | convolution fusion | flops 305528832 | bytes 8830984 | tf_op jit(solution)/shard_map/while/body/eval_jaxpr/dot_general | solution.py:83
  122.3 2.8 %fusion.154 = f32[2]{0:T(128)S(1)} fusion(f32[2,512,1024]{2,1,0:T(8,128)} %get-tuple-element.507, f32[512,512]{1,0:T(8,128)S(1)} %get-tuple-element.577), kind=kLoop, calls=%fused_computation.29.clone.1 | loop fusion | flops 2621438 | bytes 5242888 | tf_op jit(solution)/shard_map/while/body/eval_jaxpr/reduce_sum | solution.py:147
  127.8 4.6 %multiply_convert_fusion.3 = (bf16[2,512,1024]{2,1,0:T(8,128)(2,1)S(1)}, f32[2,512,1024]{2,1,0:T(8,128)}) fusion(f32[512,1024]{1,0:T(8,128)} %get-tuple-element.572, f32[2]{0:T(128)} %multiply_bitcast_fusion.2, bf16[128,1024]{1,0:T(8,128)(2,1)S(1)} %get-tuple-element.576, bf16[512,128]{1,0:T(8,128)(2,1)S(1)} %get-tuple-element.575, ...), kind=kOutput, calls=%fused_computation.25.clone.1 | convolution fusion | flops 305528832 | bytes 8830984 | tf_op jit(solution)/shard_map/while/body/eval_jaxpr/dot_general | solution.py:83
  134.3 1.4 select_add_fusion.6
  135.8 2.8 %fusion.154 = f32[2]{0:T(128)S(1)} fusion(f32[2,512,1024]{2,1,0:T(8,128)} %get-tuple-element.507, f32[512,512]{1,0:T(8,128)S(1)} %get-tuple-element.577), kind=kLoop, calls=%fused_computation.29.clone.1 | loop fusion | flops 2621438 | bytes 5242888 | tf_op jit(solution)/shard_map/while/body/eval_jaxpr/reduce_sum | solution.py:147
  141.3 4.6 %multiply_convert_fusion.3 = (bf16[2,512,1024]{2,1,0:T(8,128)(2,1)S(1)}, f32[2,512,1024]{2,1,0:T(8,128)}) fusion(f32[512,1024]{1,0:T(8,128)} %get-tuple-element.572, f32[2]{0:T(128)} %multiply_bitcast_fusion.2, bf16[128,1024]{1,0:T(8,128)(2,1)S(1)} %get-tuple-element.576, bf16[512,128]{1,0:T(8,128)(2,1)S(1)} %get-tuple-element.575, ...), kind=kOutput, calls=%fused_computation.25.clone.1 | convolution fusion | flops 305528832 | bytes 8830984 | tf_op jit(solution)/shard_map/while/body/eval_jaxpr/dot_general | solution.py:83
  147.8 1.4 select_add_fusion.6
  149.2 2.8 %fusion.154 = f32[2]{0:T(128)S(1)} fusion(f32[2,512,1024]{2,1,0:T(8,128)} %get-tuple-element.507, f32[512,512]{1,0:T(8,128)S(1)} %get-tuple-element.577), kind=kLoop, calls=%fused_computation.29.clone.1 | loop fusion | flops 2621438 | bytes 5242888 | tf_op jit(solution)/shard_map/while/body/eval_jaxpr/reduce_sum | solution.py:147
  154.8 4.6 %multiply_convert_fusion.3 = (bf16[2,512,1024]{2,1,0:T(8,128)(2,1)S(1)}, f32[2,512,1024]{2,1,0:T(8,128)}) fusion(f32[512,1024]{1,0:T(8,128)} %get-tuple-element.572, f32[2]{0:T(128)} %multiply_bitcast_fusion.2, bf16[128,1024]{1,0:T(8,128)(2,1)S(1)} %get-tuple-element.576, bf16[512,128]{1,0:T(8,128)(2,1)S(1)} %get-tuple-element.575, ...), kind=kOutput, calls=%fused_computation.25.clone.1 | convolution fusion | flops 305528832 | bytes 8830984 | tf_op jit(solution)/shard_map/while/body/eval_jaxpr/dot_general | solution.py:83
  161.3 1.4 select_add_fusion.6
  162.7 2.8 %fusion.154 = f32[2]{0:T(128)S(1)} fusion(f32[2,512,1024]{2,1,0:T(8,128)} %get-tuple-element.507, f32[512,512]{1,0:T(8,128)S(1)} %get-tuple-element.577), kind=kLoop, calls=%fused_computation.29.clone.1 | loop fusion | flops 2621438 | bytes 5242888 | tf_op jit(solution)/shard_map/while/body/eval_jaxpr/reduce_sum | solution.py:147
  168.2 4.6 %multiply_convert_fusion.3 = (bf16[2,512,1024]{2,1,0:T(8,128)(2,1)S(1)}, f32[2,512,1024]{2,1,0:T(8,128)}) fusion(f32[512,1024]{1,0:T(8,128)} %get-tuple-element.572, f32[2]{0:T(128)} %multiply_bitcast_fusion.2, bf16[128,1024]{1,0:T(8,128)(2,1)S(1)} %get-tuple-element.576, bf16[512,128]{1,0:T(8,128)(2,1)S(1)} %get-tuple-element.575, ...), kind=kOutput, calls=%fused_computation.25.clone.1 | convolution fusion | flops 305528832 | bytes 8830984 | tf_op jit(solution)/shard_map/while/body/eval_jaxpr/dot_general | solution.py:83
  176.2 2.8 %fusion.154 = f32[2]{0:T(128)S(1)} fusion(f32[2,512,1024]{2,1,0:T(8,128)} %get-tuple-element.507, f32[512,512]{1,0:T(8,128)S(1)} %get-tuple-element.577), kind=kLoop, calls=%fused_computation.29.clone.1 | loop fusion | flops 2621438 | bytes 5242888 | tf_op jit(solution)/shard_map/while/body/eval_jaxpr/reduce_sum | solution.py:147
  181.7 4.6 %multiply_convert_fusion.3 = (bf16[2,512,1024]{2,1,0:T(8,128)(2,1)S(1)}, f32[2,512,1024]{2,1,0:T(8,128)}) fusion(f32[512,1024]{1,0:T(8,128)} %get-tuple-element.572, f32[2]{0:T(128)} %multiply_bitcast_fusion.2, bf16[128,1024]{1,0:T(8,128)(2,1)S(1)} %get-tuple-element.576, bf16[512,128]{1,0:T(8,128)(2,1)S(1)} %get-tuple-element.575, ...), kind=kOutput, calls=%fused_computation.25.clone.1 | convolution fusion | flops 305528832 | bytes 8830984 | tf_op jit(solution)/shard_map/while/body/eval_jaxpr/dot_general | solution.py:83
  189.7 2.8 %fusion.154 = f32[2]{0:T(128)S(1)} fusion(f32[2,512,1024]{2,1,0:T(8,128)} %get-tuple-element.507, f32[512,512]{1,0:T(8,128)S(1)} %get-tuple-element.577), kind=kLoop, calls=%fused_computation.29.clone.1 | loop fusion | flops 2621438 | bytes 5242888 | tf_op jit(solution)/shard_map/while/body/eval_jaxpr/reduce_sum | solution.py:147
  195.2 4.6 %multiply_convert_fusion.3 = (bf16[2,512,1024]{2,1,0:T(8,128)(2,1)S(1)}, f32[2,512,1024]{2,1,0:T(8,128)}) fusion(f32[512,1024]{1,0:T(8,128)} %get-tuple-element.572, f32[2]{0:T(128)} %multiply_bitcast_fusion.2, bf16[128,1024]{1,0:T(8,128)(2,1)S(1)} %get-tuple-element.576, bf16[512,128]{1,0:T(8,128)(2,1)S(1)} %get-tuple-element.575, ...), kind=kOutput, calls=%fused_computation.25.clone.1 | convolution fusion | flops 305528832 | bytes 8830984 | tf_op jit(solution)/shard_map/while/body/eval_jaxpr/dot_general | solution.py:83
  203.2 2.8 %fusion.154 = f32[2]{0:T(128)S(1)} fusion(f32[2,512,1024]{2,1,0:T(8,128)} %get-tuple-element.507, f32[512,512]{1,0:T(8,128)S(1)} %get-tuple-element.577), kind=kLoop, calls=%fused_computation.29.clone.1 | loop fusion | flops 2621438 | bytes 5242888 | tf_op jit(solution)/shard_map/while/body/eval_jaxpr/reduce_sum | solution.py:147
  208.7 4.6 %multiply_convert_fusion.3 = (bf16[2,512,1024]{2,1,0:T(8,128)(2,1)S(1)}, f32[2,512,1024]{2,1,0:T(8,128)}) fusion(f32[512,1024]{1,0:T(8,128)} %get-tuple-element.572, f32[2]{0:T(128)} %multiply_bitcast_fusion.2, bf16[128,1024]{1,0:T(8,128)(2,1)S(1)} %get-tuple-element.576, bf16[512,128]{1,0:T(8,128)(2,1)S(1)} %get-tuple-element.575, ...), kind=kOutput, calls=%fused_computation.25.clone.1 | convolution fusion | flops 305528832 | bytes 8830984 | tf_op jit(solution)/shard_map/while/body/eval_jaxpr/dot_general | solution.py:83
  216.7 2.8 %fusion.154 = f32[2]{0:T(128)S(1)} fusion(f32[2,512,1024]{2,1,0:T(8,128)} %get-tuple-element.507, f32[512,512]{1,0:T(8,128)S(1)} %get-tuple-element.577), kind=kLoop, calls=%fused_computation.29.clone.1 | loop fusion | flops 2621438 | bytes 5242888 | tf_op jit(solution)/shard_map/while/body/eval_jaxpr/reduce_sum | solution.py:147
  220.8 11.7 %all-reduce.1 = (f32[64,64]{0,1:T(8,128)S(1)}, f32[64,64]{0,1:T(8,128)S(1)}) all-reduce(f32[64,64]{0,1:T(8,128)} %get-tuple-element.134, f32[64,64]{0,1:T(8,128)} %get-tuple-element.135), channel_id=1, replica_groups=mesh['src'=4,'tile'=8] {'src'}, use_global_device_ids=true, to_apply=%region_9.10 | all-reduce | flops 8192 | bytes 65536 | tf_op jit(solution)/shard_map/psum | solution.py:173
  233.9 1.5 fusion.120
  235.4 3.4 %collective-permute-start.2 = (bf16[64,512]{1,0:T(8,128)(2,1)S(1)}, bf16[64,512]{1,0:T(8,128)(2,1)S(1)}, u32[]{:S(2)}, u32[]{:S(2)}) collective-permute-start(bf16[64,512]{1,0:T(8,128)(2,1)S(1)} %get-tuple-element.343), channel_id=1, source_target_pairs={{0,1},{1,2},{2,3},{3,4},{4,5},{5,6},{6,7},{8,9},{9,10},{10,11},{11... | collective-permute-start | bytes 196616 | tf_op jit(solution)/shard_map/ppermute | solution.py:23
  240.2 23.1 %all-reduce = (f32[16]{0:T(128)S(1)}, f32[]{:T(128)}) all-reduce(f32[16]{0:T(128)S(1)} %reshape.193, f32[]{:T(128)} %get-tuple-element.341), channel_id=1, replica_groups=mesh['src'=4,'tile'=8] {'tile'}, use_global_device_ids=true, to_apply=%region_11.12 | all-reduce | flops 17 | bytes 136 | tf_op jit(solution)/shard_map/psum | solution.py:184
  264.7 2.5 subtract_multiply_fusion
  (259 shorter events, 55.7 us)
Async XLA Ops:
  7.2 10.5 %copy-start.12 = (s32[16,2]{0,1:T(2,128)S(1)}, s32[16,2]{0,1:T(2,128)}, u32[]{:S(2)}) copy-start(s32[16,2]{0,1:T(2,128)} %param.15) | copy-start | bytes 388
  7.2 10.7 %copy-start.13 = (f32[16]{0:T(128)S(1)}, f32[16]{0:T(128)}, u32[]{:S(2)}) copy-start(f32[16]{0:T(128)} %param.14) | copy-start | bytes 196
  7.2 102.3 %all-reduce.4.cloned.1.call-start = ((), (), s32[]{:S(2)}) async-start(), calls=%async_computation | async-start | bytes 2097152 | tf_op jit(solution)/shard_map/psum | solution.py:138
  8.8 9.5 %collective-permute-start = (bf16[64,512]{1,0:T(8,128)(2,1)S(1)}, bf16[64,512]{1,0:T(8,128)(2,1)S(1)}, u32[]{:S(2)}, u32[]{:S(2)}) collective-permute-start(bf16[64,512]{1,0:T(8,128)(2,1)S(1)} %get-tuple-element.345), channel_id=1, source_target_pairs={{0,1},{1,2},{2,3},{3,4},{4,5},{5,6},{6,7},{8,9},{9,10},{10,11},{11... | collective-permute-start | bytes 196616 | tf_op jit(solution)/shard_map/ppermute | solution.py:23
  13.6 6.2 %collective-permute-start.1 = (bf16[64,512]{1,0:T(8,128)(2,1)S(1)}, bf16[64,512]{1,0:T(8,128)(2,1)S(1)}, u32[]{:S(2)}, u32[]{:S(2)}) collective-permute-start(bf16[64,512]{1,0:T(8,128)(2,1)S(1)} %get-tuple-element.346), channel_id=1, source_target_pairs={{1,0},{2,1},{3,2},{4,3},{5,4},{6,5},{7,6},{9,8},{10,9},{11,10},{12... | collective-permute-start | bytes 196616 | tf_op jit(solution)/shard_map/ppermute | solution.py:24
  15.7 4.6 %copy-start.5 = (bf16[64,640]{1,0:T(8,128)(2,1)}, bf16[64,640]{1,0:T(8,128)(2,1)S(1)}, u32[]{:S(2)}) copy-start(bf16[64,640]{1,0:T(8,128)(2,1)S(1)} %get-tuple-element.358) | copy-start | bytes 245764
  15.7 4.6 %copy-start.6 = (bf16[64,640]{1,0:T(8,128)(2,1)}, bf16[64,640]{1,0:T(8,128)(2,1)S(1)}, u32[]{:S(2)}) copy-start(bf16[64,640]{1,0:T(8,128)(2,1)S(1)} %get-tuple-element.359) | copy-start | bytes 245764
  17.5 2.9 %copy-start.7 = (bf16[512,64]{0,1:T(8,128)(2,1)}, bf16[512,64]{0,1:T(8,128)(2,1)S(1)}, u32[]{:S(2)}) copy-start(bf16[512,64]{0,1:T(8,128)(2,1)S(1)} %get-tuple-element.354) | copy-start | bytes 196612
  17.5 2.9 %copy-start.8 = (bf16[512,64]{0,1:T(8,128)(2,1)}, bf16[512,64]{0,1:T(8,128)(2,1)S(1)}, u32[]{:S(2)}) copy-start(bf16[512,64]{0,1:T(8,128)(2,1)S(1)} %get-tuple-element.355) | copy-start | bytes 196612
  122.3 4.1 %copy-start.2 = (f32[8,2,64,64]{2,3,1,0:T(8,128)S(1)}, f32[8,2,64,64]{2,3,1,0:T(8,128)}, u32[]{:S(2)}) copy-start(f32[8,2,64,64]{2,3,1,0:T(8,128)} %copy-done.1) | copy-start | bytes 786436 | tf_op jit(solution)/shard_map/while
  122.3 4.1 %copy-start.4 = (bf16[64,64]{0,1:T(8,128)(2,1)S(1)}, bf16[64,64]{0,1:T(8,128)(2,1)}, u32[]{:S(2)}) copy-start(bf16[64,64]{0,1:T(8,128)(2,1)} %copy-done.3) | copy-start | bytes 24580 | tf_op jit(solution)/shard_map/while
  122.3 4.1 %copy-start.10 = (f32[8,2]{1,0:T(8,128)S(1)}, f32[8,2]{1,0:T(8,128)}, u32[]{:S(2)}) copy-start(f32[8,2]{1,0:T(8,128)} %copy-done.9) | copy-start | bytes 196 | tf_op jit(solution)/shard_map/while
  126.4 1.4 copy-start.1
  126.4 1.4 copy-start.3
  135.8 4.1 %copy-start.2 = (f32[8,2,64,64]{2,3,1,0:T(8,128)S(1)}, f32[8,2,64,64]{2,3,1,0:T(8,128)}, u32[]{:S(2)}) copy-start(f32[8,2,64,64]{2,3,1,0:T(8,128)} %copy-done.1) | copy-start | bytes 786436 | tf_op jit(solution)/shard_map/while
  135.8 4.1 %copy-start.4 = (bf16[64,64]{0,1:T(8,128)(2,1)S(1)}, bf16[64,64]{0,1:T(8,128)(2,1)}, u32[]{:S(2)}) copy-start(bf16[64,64]{0,1:T(8,128)(2,1)} %copy-done.3) | copy-start | bytes 24580 | tf_op jit(solution)/shard_map/while
  135.8 4.1 %copy-start.10 = (f32[8,2]{1,0:T(8,128)S(1)}, f32[8,2]{1,0:T(8,128)}, u32[]{:S(2)}) copy-start(f32[8,2]{1,0:T(8,128)} %copy-done.9) | copy-start | bytes 196 | tf_op jit(solution)/shard_map/while
  139.9 1.4 copy-start.1
  139.9 1.4 copy-start.3
  149.2 4.1 %copy-start.2 = (f32[8,2,64,64]{2,3,1,0:T(8,128)S(1)}, f32[8,2,64,64]{2,3,1,0:T(8,128)}, u32[]{:S(2)}) copy-start(f32[8,2,64,64]{2,3,1,0:T(8,128)} %copy-done.1) | copy-start | bytes 786436 | tf_op jit(solution)/shard_map/while
  149.2 4.1 %copy-start.4 = (bf16[64,64]{0,1:T(8,128)(2,1)S(1)}, bf16[64,64]{0,1:T(8,128)(2,1)}, u32[]{:S(2)}) copy-start(bf16[64,64]{0,1:T(8,128)(2,1)} %copy-done.3) | copy-start | bytes 24580 | tf_op jit(solution)/shard_map/while
  149.2 4.1 %copy-start.10 = (f32[8,2]{1,0:T(8,128)S(1)}, f32[8,2]{1,0:T(8,128)}, u32[]{:S(2)}) copy-start(f32[8,2]{1,0:T(8,128)} %copy-done.9) | copy-start | bytes 196 | tf_op jit(solution)/shard_map/while
  153.4 1.4 copy-start.1
  153.4 1.4 copy-start.3
  162.7 4.1 %copy-start.2 = (f32[8,2,64,64]{2,3,1,0:T(8,128)S(1)}, f32[8,2,64,64]{2,3,1,0:T(8,128)}, u32[]{:S(2)}) copy-start(f32[8,2,64,64]{2,3,1,0:T(8,128)} %copy-done.1) | copy-start | bytes 786436 | tf_op jit(solution)/shard_map/while
  162.7 4.1 %copy-start.4 = (bf16[64,64]{0,1:T(8,128)(2,1)S(1)}, bf16[64,64]{0,1:T(8,128)(2,1)}, u32[]{:S(2)}) copy-start(bf16[64,64]{0,1:T(8,128)(2,1)} %copy-done.3) | copy-start | bytes 24580 | tf_op jit(solution)/shard_map/while
  162.7 4.1 %copy-start.10 = (f32[8,2]{1,0:T(8,128)S(1)}, f32[8,2]{1,0:T(8,128)}, u32[]{:S(2)}) copy-start(f32[8,2]{1,0:T(8,128)} %copy-done.9) | copy-start | bytes 196 | tf_op jit(solution)/shard_map/while
  166.8 1.4 copy-start.1
  166.9 1.4 copy-start.3
  176.2 4.1 %copy-start.2 = (f32[8,2,64,64]{2,3,1,0:T(8,128)S(1)}, f32[8,2,64,64]{2,3,1,0:T(8,128)}, u32[]{:S(2)}) copy-start(f32[8,2,64,64]{2,3,1,0:T(8,128)} %copy-done.1) | copy-start | bytes 786436 | tf_op jit(solution)/shard_map/while
  176.2 4.1 %copy-start.4 = (bf16[64,64]{0,1:T(8,128)(2,1)S(1)}, bf16[64,64]{0,1:T(8,128)(2,1)}, u32[]{:S(2)}) copy-start(bf16[64,64]{0,1:T(8,128)(2,1)} %copy-done.3) | copy-start | bytes 24580 | tf_op jit(solution)/shard_map/while
  176.2 4.1 %copy-start.10 = (f32[8,2]{1,0:T(8,128)S(1)}, f32[8,2]{1,0:T(8,128)}, u32[]{:S(2)}) copy-start(f32[8,2]{1,0:T(8,128)} %copy-done.9) | copy-start | bytes 196 | tf_op jit(solution)/shard_map/while
  180.3 1.4 copy-start.1
  189.7 4.1 %copy-start.2 = (f32[8,2,64,64]{2,3,1,0:T(8,128)S(1)}, f32[8,2,64,64]{2,3,1,0:T(8,128)}, u32[]{:S(2)}) copy-start(f32[8,2,64,64]{2,3,1,0:T(8,128)} %copy-done.1) | copy-start | bytes 786436 | tf_op jit(solution)/shard_map/while
  189.7 4.1 %copy-start.4 = (bf16[64,64]{0,1:T(8,128)(2,1)S(1)}, bf16[64,64]{0,1:T(8,128)(2,1)}, u32[]{:S(2)}) copy-start(bf16[64,64]{0,1:T(8,128)(2,1)} %copy-done.3) | copy-start | bytes 24580 | tf_op jit(solution)/shard_map/while
  189.7 4.1 %copy-start.10 = (f32[8,2]{1,0:T(8,128)S(1)}, f32[8,2]{1,0:T(8,128)}, u32[]{:S(2)}) copy-start(f32[8,2]{1,0:T(8,128)} %copy-done.9) | copy-start | bytes 196 | tf_op jit(solution)/shard_map/while
  193.8 1.4 copy-start.1
  203.2 4.1 %copy-start.2 = (f32[8,2,64,64]{2,3,1,0:T(8,128)S(1)}, f32[8,2,64,64]{2,3,1,0:T(8,128)}, u32[]{:S(2)}) copy-start(f32[8,2,64,64]{2,3,1,0:T(8,128)} %copy-done.1) | copy-start | bytes 786436 | tf_op jit(solution)/shard_map/while
  203.2 4.1 %copy-start.4 = (bf16[64,64]{0,1:T(8,128)(2,1)S(1)}, bf16[64,64]{0,1:T(8,128)(2,1)}, u32[]{:S(2)}) copy-start(bf16[64,64]{0,1:T(8,128)(2,1)} %copy-done.3) | copy-start | bytes 24580 | tf_op jit(solution)/shard_map/while
  203.2 4.1 %copy-start.10 = (f32[8,2]{1,0:T(8,128)S(1)}, f32[8,2]{1,0:T(8,128)}, u32[]{:S(2)}) copy-start(f32[8,2]{1,0:T(8,128)} %copy-done.9) | copy-start | bytes 196 | tf_op jit(solution)/shard_map/while
  207.3 1.4 copy-start.1
  207.3 1.4 copy-start.3
  216.7 4.1 %copy-start.2 = (f32[8,2,64,64]{2,3,1,0:T(8,128)S(1)}, f32[8,2,64,64]{2,3,1,0:T(8,128)}, u32[]{:S(2)}) copy-start(f32[8,2,64,64]{2,3,1,0:T(8,128)} %copy-done.1) | copy-start | bytes 786436 | tf_op jit(solution)/shard_map/while
  216.7 4.1 %copy-start.4 = (bf16[64,64]{0,1:T(8,128)(2,1)S(1)}, bf16[64,64]{0,1:T(8,128)(2,1)}, u32[]{:S(2)}) copy-start(bf16[64,64]{0,1:T(8,128)(2,1)} %copy-done.3) | copy-start | bytes 24580 | tf_op jit(solution)/shard_map/while
  216.7 4.1 %copy-start.10 = (f32[8,2]{1,0:T(8,128)S(1)}, f32[8,2]{1,0:T(8,128)}, u32[]{:S(2)}) copy-start(f32[8,2]{1,0:T(8,128)} %copy-done.9) | copy-start | bytes 196 | tf_op jit(solution)/shard_map/while
  220.8 19.4 %copy-start.11 = (f32[8,2]{1,0:T(8,128)S(1)}, f32[8,2]{1,0:T(8,128)}, u32[]{:S(2)}) copy-start(f32[8,2]{1,0:T(8,128)} %get-tuple-element.136) | copy-start | bytes 196
  235.4 29.2 %collective-permute-start.2 = (bf16[64,512]{1,0:T(8,128)(2,1)S(1)}, bf16[64,512]{1,0:T(8,128)(2,1)S(1)}, u32[]{:S(2)}, u32[]{:S(2)}) collective-permute-start(bf16[64,512]{1,0:T(8,128)(2,1)S(1)} %get-tuple-element.343), channel_id=1, source_target_pairs={{0,1},{1,2},{2,3},{3,4},{4,5},{5,6},{6,7},{8,9},{9,10},{10,11},{11... | collective-permute-start | bytes 196616 | tf_op jit(solution)/shard_map/ppermute | solution.py:23
  238.8 25.8 %collective-permute-start.3 = (bf16[64,512]{1,0:T(8,128)(2,1)S(1)}, bf16[64,512]{1,0:T(8,128)(2,1)S(1)}, u32[]{:S(2)}, u32[]{:S(2)}) collective-permute-start(bf16[64,512]{1,0:T(8,128)(2,1)S(1)} %get-tuple-element.344), channel_id=1, source_target_pairs={{1,0},{2,1},{3,2},{4,3},{5,4},{6,5},{7,6},{9,8},{10,9},{11,10},{12... | collective-permute-start | bytes 196616 | tf_op jit(solution)/shard_map/ppermute | solution.py:24
  (13 other events, 17.2 us)
Sparse Core Ops, SparseCore 0:
  72.2 37.2 all-reduce.3
where the time goes:
time: 277 us; the launch traced here: 275 us
  other arithmetic  89.7 us (32%)
  matrix products  71.3 us (26%)
  waiting for transfers between devices  38.9 us (14%)
  blocking collectives  34.9 us (13%)
  between operations  16.2 us (6%)
  local copies, waits for them, and re-layouts  12.2 us (4%)
  starting transfers between devices  10.9 us (4%)
    dot_general x16, matrix products, images(): jnp.dot(row_field.reshape(source_count * tile_rows, doubled_freqs), colum...  60.1 us
    psum x1, waiting for transfers between devices, on_device(): intensity = lax.psum(partial_image, 'src')  37.4 us
    reduce_sum x8, other arithmetic, forward_step(): jnp.sum(weight_pair[:, None, None] * field_powers(fields), 0)  23.5 us
    psum x1, blocking collectives, on_device(): weight_sum, error_total = lax.psum((source_terms, error_sum), 'tile')  23.1 us
    reduce_sum x8, other arithmetic, backward_step(): source_terms = jnp.sum(cotangent[None] * field_powers(fields), axis=(1, 2))  22.5 us
    psum x1, blocking collectives, on_device(): grad_real, grad_imag = lax.psum((grads[0], grads[1]), 'src')  11.7 us
    add x8, other arithmetic, backward_step(): return ((running[0] + grad_real, running[1] + grad_imag), source_terms)  10.6 us
    dynamic_update_slice x8, local copies, waits for them, and re-layouts, on_device(): lax.scan(backward_step, (zero_spectrum, zero_spectrum), (pupil_pairs, wei...  10.2 us
  transfers between devices with their start and end apart: 5, of which 2 were waited for; matrix products, arithmetic and copies ran while one was open for 1% of the time, Pallas kernels for 0%

commit v1 on v0

v1 whole, which is shorter than its diff:
```python
import functools

import jax
import jax.numpy as jnp
import ml_dtypes
import numpy as np
from jax import lax
from jax.experimental import pallas as pl
from jax.experimental.pallas import tpu as pltpu
from jax.sharding import PartitionSpec as P

FREQS = 64
RADIUS = 20
MARGIN = 64
STEEPNESS = 12.0
THRESHOLD = 0.2

BOTH = 2 * FREQS
LANES = 128
GROUP = 4
MESH = pl.DeviceIdType.MESH
F32 = jnp.float32
BF16 = jnp.bfloat16


def angles(length_used, offset, period):
    position = np.arange(length_used, dtype=np.int64)[:, None] + offset
    frequency = np.arange(FREQS, dtype=np.int64)[None, :] - FREQS // 2
    cycles = np.mod(position * frequency, period).astype(np.float32)
    value = (cycles * np.float32(2.0 * 3.141592653589793 / period)).astype(np.float64)
    return np.cos(value).astype(np.float32), np.sin(value).astype(np.float32)


def make_tables(tile_rows, frame_rows, col_count):
    def rounded(x):
        return np.asarray(x, np.float32).astype(ml_dtypes.bfloat16)

    column_cosine, column_sine = angles(col_count, 0, col_count)
    column_forward = rounded(np.concatenate([column_cosine, -column_sine], 1))
    frame_cosine, frame_sine = angles(frame_rows, 0, frame_rows)
    row_forward = rounded(np.concatenate([frame_cosine.T, -frame_sine.T], 0))
    owned_cosine, owned_sine = angles(tile_rows, MARGIN, frame_rows)
    row_inverse = rounded(
        np.concatenate([owned_cosine, owned_sine], 1) / np.float32(frame_rows)
    )
    scale = np.float32(col_count)
    cosine_scaled, sine_scaled = column_cosine.T / scale, column_sine.T / scale
    real_part = rounded(np.concatenate([cosine_scaled, -sine_scaled], 0))
    imag_part = rounded(np.concatenate([sine_scaled, cosine_scaled], 0))
    chunks = col_count // LANES
    column_inverse = np.stack(
        [
            np.concatenate(
                [part[:, q * LANES : (q + 1) * LANES] for part in (real_part, imag_part)], 1
            )
            for q in range(chunks)
        ]
    )
    column_adjoint = np.concatenate([column_inverse[q].T for q in range(chunks)], 0)
    return (
        column_forward,
        row_forward,
        row_inverse,
        np.ascontiguousarray(row_inverse.T),
        column_inverse,
        np.ascontiguousarray(column_adjoint),
        np.concatenate([row_forward.T, row_forward.T], 1),
        np.concatenate([column_forward.T, column_forward.T], 0),
    )


def dot(a, b):
    return jnp.dot(a, b, preferred_element_type=F32)


def two_parts(x):
    high = x.astype(BF16)
    low = (x - high.astype(F32)).astype(BF16)
    return jnp.concatenate([high, low], 0)


def kernel(
    n_src,
    n_tile,
    logits_ref,
    target_ref,
    weights_ref,
    shifts_ref,
    cf_ref,
    rf_ref,
    ri_ref,
    rit_ref,
    ci_ref,
    cit_ref,
    rft_ref,
    cft_ref,
    mask_grad_ref,
    weight_grad_ref,
    loss_ref,
    target_buf,
    slope,
    params,
    wide,
    spectra,
    pupils,
    row_fields,
    fields,
    cot,
    field_grads,
    terms,
    shares,
    beside,
    stats,
    target_sem,
    param_send,
    param_recv,
    halo_send,
    halo_recv,
    share_send,
    share_recv,
    beside_send,
    beside_recv,
    stat_send,
    stat_recv,
):
    tile_rows, cols = logits_ref.shape
    local = weights_ref.shape[1]
    sources = local * n_src
    rows = tile_rows // n_src
    chunks = cols // LANES
    src = lax.axis_index("src")
    tile = lax.axis_index("tile")
    my_rows = pl.multiple_of(src * rows, rows)

    barrier = pltpu.get_barrier_semaphore()
    for d in range(1, n_src):
        pl.semaphore_signal(
            barrier, inc=1, device_id={"src": lax.rem(src + d, n_src)}, device_id_type=MESH
        )

    def greet(d, carry):
        pl.semaphore_signal(
            barrier, inc=1, device_id={"tile": lax.rem(tile + d, n_tile)}, device_id_type=MESH
        )
        return carry

    lax.fori_loop(1, n_tile, greet, 0)

    target_copy = pltpu.make_async_copy(
        target_ref.at[pl.ds(my_rows, rows)], target_buf, target_sem
    )
    target_copy.start()

    lane = lax.broadcasted_iota(jnp.int32, (local, LANES), 1)
    diagonal = lax.broadcasted_iota(jnp.int32, (local, local), 0) == lax.broadcasted_iota(
        jnp.int32, (local, local), 1
    )
    weight_column = jnp.sum(
        jnp.where(diagonal, jnp.broadcast_to(weights_ref[...], (local, local)), 0.0),
        axis=1,
        keepdims=True,
    )
    shift_values = shifts_ref[...].astype(F32)
    my_params = pl.ds(pl.multiple_of(src * local, local), local)
    params[my_params, :] = jnp.where(
        lane == 0,
        shift_values[:, 0:1],
        jnp.where(lane == 1, shift_values[:, 1:2], weight_column),
    )

    opening = jax.nn.sigmoid(logits_ref[...])
    slope[...] = opening * (1.0 - opening)
    spectra[MARGIN : MARGIN + tile_rows, :] = dot(opening.astype(BF16), cf_ref[...]).astype(BF16)

    pl.semaphore_wait(barrier, n_src - 1 + n_tile - 1)

    def param_copy(d, owner):
        slot = pl.ds(pl.multiple_of(owner * local, local), local)
        return pltpu.make_async_remote_copy(
            src_ref=params.at[slot],
            dst_ref=params.at[slot],
            send_sem=param_send.at[d],
            recv_sem=param_recv.at[owner],
            device_id={"src": lax.rem(src + d, n_src)},
            device_id_type=MESH,
        )

    for d in range(1, n_src):
        param_copy(d, src).start()

    def halo_copy(side):
        source = tile_rows if side == 0 else MARGIN
        dest = 0 if side == 0 else MARGIN + tile_rows
        return pltpu.make_async_remote_copy(
            src_ref=spectra.at[pl.ds(source, MARGIN)],
            dst_ref=spectra.at[pl.ds(dest, MARGIN)],
            send_sem=halo_send.at[side],
            recv_sem=halo_recv.at[side],
            device_id={"tile": tile + 1 if side == 0 else tile - 1},
            device_id_type=MESH,
        )

    not_first, not_last = tile > 0, tile < n_tile - 1

    @pl.when(not_last)
    def _():
        halo_copy(0).start()

    @pl.when(not_first)
    def _():
        halo_copy(1).start()

    @pl.when(tile == 0)
    def _():
        spectra[0:MARGIN, :] = jnp.zeros((MARGIN, BOTH), BF16)

    @pl.when(tile == n_tile - 1)
    def _():
        spectra[MARGIN + tile_rows :, :] = jnp.zeros((MARGIN, BOTH), BF16)

    for d in range(1, n_src):
        param_copy(d, lax.rem(src + n_src - d, n_src)).wait_recv()

    for k in range(3):
        wide[k] = jnp.broadcast_to(params[:, k : k + 1], (sources, LANES))

    frequency_row = (
        lax.rem(lax.broadcasted_iota(jnp.int32, (FREQS, BOTH), 0), FREQS) - FREQS // 2
    ).astype(F32)
    frequency_lane = (
        lax.rem(lax.broadcasted_iota(jnp.int32, (1, BOTH), 1), FREQS) - FREQS // 2
    ).astype(F32)

    @pl.when(not_first)
    def _():
        halo_copy(0).wait_recv()

    @pl.when(not_last)
    def _():
        halo_copy(1).wait_recv()

    half_sign = jnp.where(lax.broadcasted_iota(jnp.int32, (1, BOTH), 1) < FREQS, 1.0, -1.0)
    product = dot(rf_ref[...], spectra[...])
    turned = pltpu.roll(product, FREQS, 1)
    block_top = product[:FREQS] - half_sign * turned[FREQS:]
    block_low = -product[FREQS:] - half_sign * turned[:FREQS]
    inverse_rows = ri_ref[pl.ds(my_rows, rows), :]

    def row_step(pair, carry):
        blocks = []
        for i in range(2):
            s = pair * 2 + i
            along = frequency_row - wide[0, pl.ds(s, 1), :]
            across = frequency_lane - wide[1, pl.ds(s, 1), :]
            inside = along * along + across * across <= float(RADIUS * RADIUS)
            pupils[s] = jnp.where(inside, 1.0, 0.0)
            blocks.append(
                jnp.concatenate(
                    [jnp.where(inside, block_top, 0.0), jnp.where(inside, block_low, 0.0)], 0
                ).astype(BF16)
            )
        both = dot(inverse_rows, jnp.concatenate(blocks, 1)).astype(BF16)
        for i in range(2):
            start = pl.multiple_of((pair * 2 + i) * rows, rows)
            row_fields[pl.ds(start, rows), :] = both[:, i * BOTH : (i + 1) * BOTH]
        return carry

    lax.fori_loop(0, sources // 2, row_step, 0, unroll=2)

    target_copy.wait()
    span = GROUP * rows
    error_sum = jnp.zeros((1, LANES), F32)
    for q in range(chunks):
        inverse_chunk = ci_ref[q]

        def field_step(group, image, q=q, inverse_chunk=inverse_chunk):
            place = pl.ds(pl.multiple_of(group * span, span), span)
            values = dot(row_fields[place, :], inverse_chunk)
            fields[q, place, :] = values
            real, imag = values[:, :LANES], values[:, LANES:]
            power = real * real + imag * imag
            for i in range(GROUP):
                weight = wide[2, pl.ds(group * GROUP + i, 1), :]
                image = image + weight * power[i * rows : (i + 1) * rows]
            return image

        image = lax.fori_loop(0, sources // GROUP, field_step, jnp.zeros((rows, LANES), F32))
        printed = jax.nn.sigmoid(STEEPNESS * (image - THRESHOLD))
        wanted = target_buf[:, q * LANES : (q + 1) * LANES].astype(F32)
        error = printed - wanted
        cot[q] = 2.0 * STEEPNESS * error * printed * (1.0 - printed)
        error_sum = error_sum + jnp.sum(error * error, axis=0, keepdims=True)

    adjoint_rows = rit_ref[:, pl.ds(my_rows, rows)]

    def grad_step(group, carry):
        place = pl.ds(pl.multiple_of(group * span, span), span)
        for i in range(GROUP):
            s = group * GROUP + i
            doubled_weight = 2.0 * wide[2, pl.ds(s, 1), :]
            total = jnp.zeros((8, LANES), F32)
            for q in range(chunks):
                part = fields[q, pl.ds(pl.multiple_of(s * rows, rows), rows), :]
                real, imag = part[:, :LANES], part[:, LANES:]
                scaling = doubled_weight * cot[q]
                real_grad, imag_grad = scaling * real, scaling * imag
                term = real_grad * real + imag_grad * imag
                total = total + jnp.sum(term.reshape(rows // 8, 8, LANES), axis=0)
                at = slice(i * rows, (i + 1) * rows)
                field_grads[at, 2 * q * LANES : (2 * q + 1) * LANES] = real_grad.astype(BF16)
                field_grads[at, (2 * q + 1) * LANES : (2 * q + 2) * LANES] = imag_grad.astype(BF16)
            terms[pl.ds(s, 1), :] = jnp.sum(total, axis=0, keepdims=True)
        row_grad = dot(field_grads[...], cit_ref[...]).astype(BF16)
        top, low = carry
        for pair in range(GROUP // 2):
            begin = 2 * pair * rows
            block_grad = dot(
                adjoint_rows,
                jnp.concatenate(
                    [row_grad[begin : begin + rows], row_grad[begin + rows : begin + 2 * rows]], 1
                ),
            )
            for i in range(2):
                pupil = pupils[group * GROUP + 2 * pair + i]
                one = block_grad[:, i * BOTH : (i + 1) * BOTH]
                top = top + pupil * one[:FREQS]
                low = low + pupil * one[FREQS:]
        return top, low

    zero = jnp.zeros((FREQS, BOTH), F32)
    top, low = lax.fori_loop(0, sources // GROUP, grad_step, (zero, zero))

    shares[src, 0:FREQS, :] = top + half_sign * pltpu.roll(low, FREQS, 1)
    source_column = jnp.sum(terms[...], axis=1, keepdims=True) / (2.0 * wide[2, :, 0:1])
    source_lane = lax.broadcasted_iota(jnp.int32, (sources, LANES), 1)
    source_row = lax.broadcasted_iota(jnp.int32, (sources, LANES), 0)
    sums = jnp.sum(jnp.where(source_lane == source_row, source_column, 0.0), axis=0, keepdims=True)
    error_total = jnp.sum(error_sum, axis=1, keepdims=True)
    first_lane = lax.broadcasted_iota(jnp.int32, (8, LANES), 1)
    first_row = lax.broadcasted_iota(jnp.int32, (8, LANES), 0)
    shares[src, FREQS : FREQS + 8, :] = jnp.where(
        first_row == 0, sums, jnp.where(first_lane == 0, error_total, 0.0)
    )

    def share_copy(d, owner):
        return pltpu.make_async_remote_copy(
            src_ref=shares.at[owner],
            dst_ref=shares.at[owner],
            send_sem=share_send.at[d],
            recv_sem=share_recv.at[owner],
            device_id={"src": lax.rem(src + d, n_src)},
            device_id_type=MESH,
        )

    for d in range(1, n_src):
        share_copy(d, src).start()
    for d in range(1, n_src):
        share_copy(d, lax.rem(src + n_src - d, n_src)).wait_recv()

    whole = shares[0]
    for i in range(1, n_src):
        whole = whole + shares[i]
    beside[2] = whole[:FREQS]
    stats[tile] = whole[FREQS:]

    def beside_copy(side):
        return pltpu.make_async_remote_copy(
            src_ref=beside.at[2],
            dst_ref=beside.at[side],
            send_sem=beside_send.at[side],
            recv_sem=beside_recv.at[side],
            device_id={"tile": tile + 1 if side == 0 else tile - 1},
            device_id_type=MESH,
        )

    @pl.when(not_last)
    def _():
        beside_copy(0).start()

    @pl.when(not_first)
    def _():
        beside_copy(1).start()

    @pl.when(tile == 0)
    def _():
        beside[0] = jnp.zeros((FREQS, BOTH), F32)

    @pl.when(tile == n_tile - 1)
    def _():
        beside[1] = jnp.zeros((FREQS, BOTH), F32)

    def stat_copy(d, owner):
        return pltpu.make_async_remote_copy(
            src_ref=stats.at[owner],
            dst_ref=stats.at[owner],
            send_sem=stat_send.at[d],
            recv_sem=stat_recv.at[owner],
            device_id={"tile": lax.rem(tile + d, n_tile)},
            device_id_type=MESH,
        )

    def start_stat(d, carry):
        stat_copy(d, tile).start()
        return carry

    lax.fori_loop(1, n_tile, start_stat, 0)

    def doubled(half):
        return two_parts(jnp.concatenate([half, half_sign * pltpu.roll(half, FREQS, 1)], 0))

    frame_rows = tile_rows + 2 * MARGIN
    column_grad = dot(rft_ref[MARGIN : MARGIN + tile_rows, :], doubled(whole[:FREQS]))

    @pl.when(not_first)
    def _():
        beside_copy(0).wait_recv()

    @pl.when(not_last)
    def _():
        beside_copy(1).wait_recv()

    before = dot(rft_ref[frame_rows - MARGIN : frame_rows, :], doubled(beside[0]))
    after = dot(rft_ref[0:MARGIN, :], doubled(beside[1]))
    column_grad = jnp.concatenate(
        [
            column_grad[:MARGIN] + before,
            column_grad[MARGIN : tile_rows - MARGIN],
            column_grad[tile_rows - MARGIN :] + after,
        ],
        0,
    )
    high = column_grad.astype(BF16)
    low_part = (column_grad - high.astype(F32)).astype(BF16)
    mask_grad_ref[...] = (
        dot(jnp.concatenate([high, low_part], 1), cft_ref[...]) * slope[...]
    )

    def wait_stat(d, carry):
        stat_copy(d, lax.rem(tile + n_tile - d, n_tile)).wait_recv()
        return carry

    lax.fori_loop(1, n_tile, wait_stat, 0)
    total = jnp.sum(stats[...], axis=0)
    pixels = float(tile_rows * cols * n_tile)
    picked = lax.broadcasted_iota(jnp.int32, (sources, local), 0) == (
        lax.broadcasted_iota(jnp.int32, (sources, local), 1) + src * local
    )
    total_column = jnp.sum(
        jnp.where(source_lane == source_row, total[0:1, :], 0.0), axis=1, keepdims=True
    )
    weight_grad_ref[...] = (
        jnp.sum(jnp.where(picked, total_column, 0.0), axis=0, keepdims=True) / pixels
    )
    loss_ref[...] = total[1:2, 0:1] / pixels

    for d in range(1, n_src):
        param_copy(d, src).wait_send()
        share_copy(d, src).wait_send()

    @pl.when(not_last)
    def _():
        halo_copy(0).wait_send()
        beside_copy(0).wait_send()

    @pl.when(not_first)
    def _():
        halo_copy(1).wait_send()
        beside_copy(1).wait_send()

    def end_stat(d, carry):
        stat_copy(d, tile).wait_send()
        return carry

    lax.fori_loop(1, n_tile, end_stat, 0)


def on_device(n_src, n_tile, mask_logits, target, weights, shifts):
    tile_rows, cols = mask_logits.shape
    local = weights.shape[0]
    sources = local * n_src
    rows = tile_rows // n_src
    chunks = cols // LANES
    frame_rows = tile_rows + 2 * MARGIN
    tables = make_tables(tile_rows, frame_rows, cols)
    vmem = pl.BlockSpec(memory_space=pltpu.VMEM)
    dma = pltpu.SemaphoreType.DMA
    mask_grad, weight_grad, loss = pl.pallas_call(
        functools.partial(kernel, n_src, n_tile),
        out_shape=(
            jax.ShapeDtypeStruct((tile_rows, cols), F32),
            jax.ShapeDtypeStruct((1, local), F32),
            jax.ShapeDtypeStruct((1, 1), F32),
        ),
        in_specs=[vmem, pl.BlockSpec(memory_space=pl.ANY)] + [vmem] * (2 + len(tables)),
        out_specs=(vmem, vmem, vmem),
        scratch_shapes=[
            pltpu.VMEM((rows, cols), jnp.int32),
            pltpu.VMEM((tile_rows, cols), F32),
            pltpu.VMEM((sources, LANES), F32),
            pltpu.VMEM((3, sources, LANES), F32),
            pltpu.VMEM((frame_rows, BOTH), BF16),
            pltpu.VMEM((sources, FREQS, BOTH), F32),
            pltpu.VMEM((sources * rows, BOTH), BF16),
            pltpu.VMEM((chunks, sources * rows, 2 * LANES), F32),
            pltpu.VMEM((chunks, rows, LANES), F32),
            pltpu.VMEM((GROUP * rows, 2 * cols), BF16),
            pltpu.VMEM((sources, LANES), F32),
            pltpu.VMEM((n_src, FREQS + 8, BOTH), F32),
            pltpu.VMEM((3, FREQS, BOTH), F32),
            pltpu.VMEM((n_tile, 8, LANES), F32),
            dma,
            dma((n_src,)),
            dma((n_src,)),
            dma((2,)),
            dma((2,)),
            dma((n_src,)),
            dma((n_src,)),
            dma((2,)),
            dma((2,)),
            dma((n_tile,)),
            dma((n_tile,)),
        ],
        compiler_params=pltpu.CompilerParams(
            collective_id=0, has_side_effects=True, vmem_limit_bytes=56 * 1024 * 1024
        ),
    )(mask_logits, target, weights.reshape(1, local), shifts, *[jnp.asarray(t) for t in tables])
    return mask_grad, weight_grad.reshape(local), loss.reshape(())


def solution(mesh):
    placed = (P("tile", None), P("tile", None), P("src"), P("src", None))
    return jax.shard_map(
        functools.partial(on_device, mesh.shape["src"], mesh.shape["tile"]),
        mesh=mesh,
        in_specs=placed,
        out_specs=(P("tile", None), P("src"), P()),
        check_vma=False,
    )
```

time: 277 us -> 57.1 us (0.21)
  other arithmetic: 89.7 us -> 0 us
  matrix products: 71.3 us -> 0 us
  Pallas kernels: 0 us -> 50.5 us
  waiting for transfers between devices: 38.9 us -> 0 us
  blocking collectives: 34.9 us -> 0 us
  between operations: 16.2 us -> 2.35 us
  starting transfers between devices: 10.9 us -> 0 us
  local copies, waits for them, and re-layouts: 12.2 us -> 4.13 us
    dot_general x35 -> x0, matrix products: 71.3 us -> none  [the longest x16 60.1 us: images(): jnp.dot(row_field.reshape(source_count * tile_rows, doubled_freqs), colum...]
    reduce_sum x25 -> x0, other arithmetic: 56.2 us -> none  [the longest x8 23.5 us: forward_step(): jnp.sum(weight_pair[:, None, None] * field_powers(fields), 0)]
    pallas_call x0 -> x1, Pallas kernels: none -> 50.5 us  [on_device(): pl.pallas_call(functools.partial(kernel, n_src, n_tile), out_shape=(jax.S...]
    psum x1 -> x0, waiting for transfers between devices: 37.4 us -> none  [on_device(): intensity = lax.psum(partial_image, 'src')]
    psum x2 -> x0, blocking collectives: 34.9 us -> none  [the longest x1 23.1 us: on_device(): weight_sum, error_total = lax.psum((source_terms, error_sum), 'tile')]
    add x17 -> x0, other arithmetic: 13.5 us -> none  [the longest x8 10.6 us: backward_step(): return ((running[0] + grad_real, running[1] + grad_imag), source_terms)]
    ppermute x4 -> x0, starting transfers between devices: 10.8 us -> none  [the longest x2 8.26 us: extended(): before = lax.ppermute(last, axis, up)]
    dynamic_update_slice x8 -> x0, local copies, waits for them, and re-layouts: 10.2 us -> none  [on_device(): lax.scan(backward_step, (zero_spectrum, zero_spectrum), (pupil_pairs, wei...]
  transfers between devices with their start and end apart: 5 -> 0, of which waited for: 2 -> 0; matrix products, arithmetic and copies ran while one was open for 1% -> 0% of each run, Pallas kernels for 0% -> 0%
where the time goes in v1:
time: 57.1 us; the launch traced here: 56.9 us
  Pallas kernels  50.5 us (88%)
  local copies, waits for them, and re-layouts  4.13 us (7%)
  between operations  2.35 us (4%)
    pallas_call x1, Pallas kernels, on_device(): pl.pallas_call(functools.partial(kernel, n_src, n_tile), out_shape=(jax.S...  50.5 us
    unnamed x7, local copies, waits for them, and re-layouts  4.13 us

profile of v1, /device:TPU:0, one launch (start us, length us, event | category | flops | bytes accessed | tf_op | source)
XLA Modules:
  0.0 56.9 jit_solution(1221061311424657368)
XLA Ops:
  0.6 0.0 copy-start
  0.6 0.7 %copy-done = s32[16,2]{0,1:T(2,128)S(1)} copy-done((s32[16,2]{0,1:T(2,128)S(1)}, s32[16,2]{0,1:T(2,128)}, u32[]{:S(2)}) %copy-start) | copy-done | bytes 152
  1.3 0.7 %copy.15.shifts_ref = s32[16,2]{1,0:T(8,128)} copy(s32[16,2]{0,1:T(2,128)S(1)} %copy-done) | data formatting | bytes 256 | tf_op args[3]
  2.0 50.5 %shard_map.139 = (f32[512,512]{1,0:T(8,128)}, f32[1,16]{1,0:T(1,128)}, f32[1,1]{1,0:T(1,128)}) custom-call(f32[512,512]{1,0:T(8,128)} %logits_ref.1, s32[512,512]{1,0:T(8,128)} %target_ref.1, f32[1,16]{1,0:T(1,128)} %bitcast.3, s32[16,2]{1,0:T(8,128)} %copy.15.shifts_ref, bf16[512,128]{1,0:T(8,128)(2,1)} %constant.16.clone.cf_ref, ...), custom_call_target="tpu_custom_call" | custom-call | tf_op jit(solution)/shard_map/pallas_call | solution.py:487
  52.5 0.0 copy-start.1
  52.5 2.3 %copy.19 = f32[512,512]{1,0:T(8,128)} copy(f32[512,512]{1,0:T(8,128)} %get-tuple-element.12) | data formatting | bytes 2097152
  54.7 0.0 copy-done.1
  54.7 0.5 copy.20
Async XLA Ops:
  0.6 0.7 %copy-start = (s32[16,2]{0,1:T(2,128)S(1)}, s32[16,2]{0,1:T(2,128)}, u32[]{:S(2)}) copy-start(s32[16,2]{0,1:T(2,128)} %param.15) | copy-start | bytes 388
  52.5 2.3 %copy-start.1 = (f32[1,16]{1,0:T(1,128)S(1)}, f32[1,16]{1,0:T(1,128)}, u32[]{:S(2)}) copy-start(f32[1,16]{1,0:T(1,128)} %get-tuple-element.7) | copy-start | bytes 196

commit v2 on v1

--- a/solution.py
+++ b/solution.py
@@ -82,10 +82,21 @@
 def kernel(
     n_src,
     n_tile,
-    logits_ref,
+    logits_hbm,
     target_ref,
     weights_ref,
     shifts_ref,
+    cf_hbm,
+    rf_hbm,
+    ri_hbm,
+    rit_hbm,
+    ci_hbm,
+    cit_hbm,
+    rft_hbm,
+    column_grad_ref,
+    weight_grad_ref,
+    loss_ref,
+    logits_ref,
     cf_ref,
     rf_ref,
     ri_ref,
@@ -93,12 +104,7 @@
     ci_ref,
     cit_ref,
     rft_ref,
-    cft_ref,
-    mask_grad_ref,
-    weight_grad_ref,
-    loss_ref,
     target_buf,
-    slope,
     params,
     wide,
     spectra,
@@ -106,11 +112,13 @@
     row_fields,
     fields,
     cot,
-    field_grads,
+    even_grads,
+    odd_grads,
     terms,
     shares,
     beside,
     stats,
+    input_sem,
     target_sem,
     param_send,
     param_recv,
@@ -123,7 +131,7 @@
     stat_send,
     stat_recv,
 ):
-    tile_rows, cols = logits_ref.shape
+    tile_rows, cols = logits_hbm.shape
     local = weights_ref.shape[1]
     sources = local * n_src
     rows = tile_rows // n_src
@@ -146,6 +154,23 @@
 
     lax.fori_loop(1, n_tile, greet, 0)
 
+    inputs = [
+        pltpu.make_async_copy(source, dest, input_sem.at[i])
+        for i, (source, dest) in enumerate(
+            [
+                (logits_hbm, logits_ref),
+                (cf_hbm, cf_ref),
+                (rf_hbm, rf_ref),
+                (ri_hbm.at[pl.ds(my_rows, rows)], ri_ref),
+                (ci_hbm, ci_ref),
+                (rit_hbm, rit_ref),
+                (cit_hbm, cit_ref),
+                (rft_hbm, rft_ref),
+            ]
+        )
+    ]
+    for copy in inputs:
+        copy.start()
     target_copy = pltpu.make_async_copy(
         target_ref.at[pl.ds(my_rows, rows)], target_buf, target_sem
     )
@@ -155,23 +180,18 @@
     diagonal = lax.broadcasted_iota(jnp.int32, (local, local), 0) == lax.broadcasted_iota(
         jnp.int32, (local, local), 1
     )
-    weight_column = jnp.sum(
-        jnp.where(diagonal, jnp.broadcast_to(weights_ref[...], (local, local)), 0.0),
-        axis=1,
-        keepdims=True,
-    )
+
+    def column(row):
+        spread = jnp.where(diagonal, jnp.broadcast_to(row, (local, local)), 0.0)
+        return jnp.sum(spread, axis=1, keepdims=True)
+
     shift_values = shifts_ref[...].astype(F32)
     my_params = pl.ds(pl.multiple_of(src * local, local), local)
     params[my_params, :] = jnp.where(
         lane == 0,
-        shift_values[:, 0:1],
-        jnp.where(lane == 1, shift_values[:, 1:2], weight_column),
-    )
-
-    opening = jax.nn.sigmoid(logits_ref[...])
-    slope[...] = opening * (1.0 - opening)
-    spectra[MARGIN : MARGIN + tile_rows, :] = dot(opening.astype(BF16), cf_ref[...]).astype(BF16)
-
+        column(shift_values[0:1, :]),
+        jnp.where(lane == 1, column(shift_values[1:2, :]), column(weights_ref[...])),
+    )
     pl.semaphore_wait(barrier, n_src - 1 + n_tile - 1)
 
     def param_copy(d, owner):
@@ -187,6 +207,11 @@
 
     for d in range(1, n_src):
         param_copy(d, src).start()
+
+    inputs[0].wait()
+    inputs[1].wait()
+    opening = jax.nn.sigmoid(logits_ref[...]).astype(BF16)
+    spectra[MARGIN : MARGIN + tile_rows, :] = dot(opening, cf_ref[...]).astype(BF16)
 
     def halo_copy(side):
         source = tile_rows if side == 0 else MARGIN
@@ -231,6 +256,17 @@
         lax.rem(lax.broadcasted_iota(jnp.int32, (1, BOTH), 1), FREQS) - FREQS // 2
     ).astype(F32)
 
+    def pupil_step(s, carry):
+        along = frequency_row - wide[0, pl.ds(s, 1), :]
+        across = frequency_lane - wide[1, pl.ds(s, 1), :]
+        inside = along * along + across * across <= float(RADIUS * RADIUS)
+        pupils[s] = jnp.where(inside, 1.0, 0.0)
+        return carry
+
+    lax.fori_loop(0, sources, pupil_step, 0, unroll=4)
+    for copy in inputs[2:5]:
+        copy.wait()
+
     @pl.when(not_first)
     def _():
         halo_copy(0).wait_recv()
@@ -244,20 +280,14 @@
     turned = pltpu.roll(product, FREQS, 1)
     block_top = product[:FREQS] - half_sign * turned[FREQS:]
     block_low = -product[FREQS:] - half_sign * turned[:FREQS]
-    inverse_rows = ri_ref[pl.ds(my_rows, rows), :]
+    inverse_rows = ri_ref[...]
 
     def row_step(pair, carry):
         blocks = []
         for i in range(2):
-            s = pair * 2 + i
-            along = frequency_row - wide[0, pl.ds(s, 1), :]
-            across = frequency_lane - wide[1, pl.ds(s, 1), :]
-            inside = along * along + across * across <= float(RADIUS * RADIUS)
-            pupils[s] = jnp.where(inside, 1.0, 0.0)
+            pupil = pupils[pair * 2 + i]
             blocks.append(
-                jnp.concatenate(
-                    [jnp.where(inside, block_top, 0.0), jnp.where(inside, block_low, 0.0)], 0
-                ).astype(BF16)
+                jnp.concatenate([pupil * block_top, pupil * block_low], 0).astype(BF16)
             )
         both = dot(inverse_rows, jnp.concatenate(blocks, 1)).astype(BF16)
         for i in range(2):
@@ -265,7 +295,7 @@
             row_fields[pl.ds(start, rows), :] = both[:, i * BOTH : (i + 1) * BOTH]
         return carry
 
-    lax.fori_loop(0, sources // 2, row_step, 0, unroll=2)
+    lax.fori_loop(0, sources // 2, row_step, 0, unroll=4)
 
     target_copy.wait()
     span = GROUP * rows
@@ -284,17 +314,20 @@
                 image = image + weight * power[i * rows : (i + 1) * rows]
             return image
 
-        image = lax.fori_loop(0, sources // GROUP, field_step, jnp.zeros((rows, LANES), F32))
+        image = lax.fori_loop(
+            0, sources // GROUP, field_step, jnp.zeros((rows, LANES), F32), unroll=4
+        )
         printed = jax.nn.sigmoid(STEEPNESS * (image - THRESHOLD))
         wanted = target_buf[:, q * LANES : (q + 1) * LANES].astype(F32)
         error = printed - wanted
         cot[q] = 2.0 * STEEPNESS * error * printed * (1.0 - printed)
         error_sum = error_sum + jnp.sum(error * error, axis=0, keepdims=True)
 
+    for copy in inputs[5:]:
+        copy.wait()
     adjoint_rows = rit_ref[:, pl.ds(my_rows, rows)]
 
-    def grad_step(group, carry):
-        place = pl.ds(pl.multiple_of(group * span, span), span)
+    def weigh(group, grads):
         for i in range(GROUP):
             s = group * GROUP + i
             doubled_weight = 2.0 * wide[2, pl.ds(s, 1), :]
@@ -307,10 +340,12 @@
                 term = real_grad * real + imag_grad * imag
                 total = total + jnp.sum(term.reshape(rows // 8, 8, LANES), axis=0)
                 at = slice(i * rows, (i + 1) * rows)
-                field_grads[at, 2 * q * LANES : (2 * q + 1) * LANES] = real_grad.astype(BF16)
-                field_grads[at, (2 * q + 1) * LANES : (2 * q + 2) * LANES] = imag_grad.astype(BF16)
-            terms[pl.ds(s, 1), :] = jnp.sum(total, axis=0, keepdims=True)
-        row_grad = dot(field_grads[...], cit_ref[...]).astype(BF16)
+                grads[at, 2 * q * LANES : (2 * q + 1) * LANES] = real_grad.astype(BF16)
+                grads[at, (2 * q + 1) * LANES : (2 * q + 2) * LANES] = imag_grad.astype(BF16)
+            terms[s] = total
+
+    def adjoint(group, grads, carry):
+        row_grad = dot(grads[...], cit_ref[...]).astype(BF16)
         top, low = carry
         for pair in range(GROUP // 2):
             begin = 2 * pair * rows
@@ -327,11 +362,24 @@
                 low = low + pupil * one[FREQS:]
         return top, low
 
+    def grad_step(step, carry):
+        weigh(2 * step + 1, odd_grads)
+        carry = adjoint(2 * step, even_grads, carry)
+        weigh(2 * step + 2, even_grads)
+        return adjoint(2 * step + 1, odd_grads, carry)
+
+    groups = sources // GROUP
     zero = jnp.zeros((FREQS, BOTH), F32)
-    top, low = lax.fori_loop(0, sources // GROUP, grad_step, (zero, zero))
+    weigh(0, even_grads)
+    carry = lax.fori_loop(0, groups // 2 - 1, grad_step, (zero, zero))
+    weigh(groups - 1, odd_grads)
+    carry = adjoint(groups - 2, even_grads, carry)
+    top, low = adjoint(groups - 1, odd_grads, carry)
 
     shares[src, 0:FREQS, :] = top + half_sign * pltpu.roll(low, FREQS, 1)
-    source_column = jnp.sum(terms[...], axis=1, keepdims=True) / (2.0 * wide[2, :, 0:1])
+    source_column = jnp.sum(jnp.sum(terms[...], axis=1), axis=1, keepdims=True) / (
+        2.0 * wide[2, :, 0:1]
+    )
     source_lane = lax.broadcasted_iota(jnp.int32, (sources, LANES), 1)
     source_row = lax.broadcasted_iota(jnp.int32, (sources, LANES), 0)
     sums = jnp.sum(jnp.where(source_lane == source_row, source_column, 0.0), axis=0, keepdims=True)
@@ -430,10 +478,8 @@
         0,
     )
     high = column_grad.astype(BF16)
-    low_part = (column_grad - high.astype(F32)).astype(BF16)
-    mask_grad_ref[...] = (
-        dot(jnp.concatenate([high, low_part], 1), cft_ref[...]) * slope[...]
-    )
+    column_grad_ref[:, :BOTH] = high
+    column_grad_ref[:, BOTH:] = (column_grad - high.astype(F32)).astype(BF16)
 
     def wait_stat(d, carry):
         stat_copy(d, lax.rem(tile + n_tile - d, n_tile)).wait_recv()
@@ -472,6 +518,13 @@
         return carry
 
     lax.fori_loop(1, n_tile, end_stat, 0)
+
+
+def last_kernel(column_grad, logits, cft, weight_in, loss_in, mask_grad, weight_grad, loss):
+    opening = jax.nn.sigmoid(logits[...])
+    mask_grad[...] = dot(column_grad[...], cft[...]) * opening * (1.0 - opening)
+    weight_grad[...] = weight_in[...]
+    loss[...] = loss_in[...]
 
 
 def on_device(n_src, n_tile, mask_logits, target, weights, shifts):
@@ -481,21 +534,23 @@
     rows = tile_rows // n_src
     chunks = cols // LANES
     frame_rows = tile_rows + 2 * MARGIN
-    tables = make_tables(tile_rows, frame_rows, cols)
+    tables = [jnp.asarray(t) for t in make_tables(tile_rows, frame_rows, cols)]
+    last_table = tables.pop()
     vmem = pl.BlockSpec(memory_space=pltpu.VMEM)
+    hbm = pl.BlockSpec(memory_space=pl.ANY)
     dma = pltpu.SemaphoreType.DMA
-    mask_grad, weight_grad, loss = pl.pallas_call(
+    buffers = [pltpu.VMEM(t.shape, BF16) for t in tables]
+    buffers[2] = pltpu.VMEM((rows, BOTH), BF16)
+    small = (jax.ShapeDtypeStruct((1, local), F32), jax.ShapeDtypeStruct((1, 1), F32))
+    column_grad, weight_grad, loss = pl.pallas_call(
         functools.partial(kernel, n_src, n_tile),
-        out_shape=(
-            jax.ShapeDtypeStruct((tile_rows, cols), F32),
-            jax.ShapeDtypeStruct((1, local), F32),
-            jax.ShapeDtypeStruct((1, 1), F32),
-        ),
-        in_specs=[vmem, pl.BlockSpec(memory_space=pl.ANY)] + [vmem] * (2 + len(tables)),
+        out_shape=(jax.ShapeDtypeStruct((tile_rows, 2 * BOTH), BF16),) + small,
+        in_specs=[hbm, hbm, vmem, vmem] + [hbm] * len(tables),
         out_specs=(vmem, vmem, vmem),
-        scratch_shapes=[
+        scratch_shapes=[pltpu.VMEM((tile_rows, cols), F32)]
+        + buffers
+        + [
             pltpu.VMEM((rows, cols), jnp.int32),
-            pltpu.VMEM((tile_rows, cols), F32),
             pltpu.VMEM((sources, LANES), F32),
             pltpu.VMEM((3, sources, LANES), F32),
             pltpu.VMEM((frame_rows, BOTH), BF16),
@@ -504,10 +559,12 @@
             pltpu.VMEM((chunks, sources * rows, 2 * LANES), F32),
             pltpu.VMEM((chunks, rows, LANES), F32),
             pltpu.VMEM((GROUP * rows, 2 * cols), BF16),
-            pltpu.VMEM((sources, LANES), F32),
+            pltpu.VMEM((GROUP * rows, 2 * cols), BF16),
+            pltpu.VMEM((sources, 8, LANES), F32),
             pltpu.VMEM((n_src, FREQS + 8, BOTH), F32),
             pltpu.VMEM((3, FREQS, BOTH), F32),
             pltpu.VMEM((n_tile, 8, LANES), F32),
+            dma((1 + len(tables),)),
             dma,
             dma((n_src,)),
             dma((n_src,)),
@@ -523,7 +580,22 @@
         compiler_params=pltpu.CompilerParams(
             collective_id=0, has_side_effects=True, vmem_limit_bytes=56 * 1024 * 1024
         ),
-    )(mask_logits, target, weights.reshape(1, local), shifts, *[jnp.asarray(t) for t in tables])
+    )(mask_logits, target, weights.reshape(1, local), shifts.T, *tables)
+    steps = 4
+    block = tile_rows // steps
+    whole_small = [pl.BlockSpec(x.shape, lambda i: (0, 0)) for x in small]
+    mask_grad, weight_grad, loss = pl.pallas_call(
+        last_kernel,
+        grid=(steps,),
+        out_shape=(jax.ShapeDtypeStruct((tile_rows, cols), F32),) + small,
+        in_specs=[
+            pl.BlockSpec((block, 2 * BOTH), lambda i: (i, 0)),
+            pl.BlockSpec((block, cols), lambda i: (i, 0)),
+            pl.BlockSpec((2 * BOTH, cols), lambda i: (0, 0)),
+        ]
+        + whole_small,
+        out_specs=tuple([pl.BlockSpec((block, cols), lambda i: (i, 0))] + whole_small),
+    )(column_grad, mask_logits, last_table, weight_grad, loss)
     return mask_grad, weight_grad.reshape(local), loss.reshape(())
 
 

time: 57.1 us -> 46.4 us (0.81)
  Pallas kernels: 50.5 us -> 45.6 us
  local copies, waits for them, and re-layouts: 4.13 us -> 0 us
  between operations: 2.35 us -> 0.64 us
    pallas_call x1, Pallas kernels: 50.5 us -> 41 us  [on_device(): pl.pallas_call(functools.partial(kernel, n_src, n_tile), out_shape=(jax.S...]
    pallas_call x0 -> x1, Pallas kernels: none -> 4.58 us  [on_device(): pl.pallas_call(last_kernel, grid=(steps,), out_shape=(jax.ShapeDtypeStruc...]
    unnamed x7 -> x0, local copies, waits for them, and re-layouts: 4.13 us -> none
where the time goes in v2:
time: 46.4 us; the launch traced here: 46.2 us
  Pallas kernels  45.6 us (98%)
  between operations  0.64 us (1%)
    pallas_call x1, Pallas kernels, on_device(): pl.pallas_call(functools.partial(kernel, n_src, n_tile), out_shape=(jax.S...  41 us
    pallas_call x1, Pallas kernels, on_device(): pl.pallas_call(last_kernel, grid=(steps,), out_shape=(jax.ShapeDtypeStruc...  4.58 us

profile of v2, /device:TPU:0, one launch (start us, length us, event | category | flops | bytes accessed | tf_op | source)
XLA Modules:
  0.0 46.2 jit_solution(15945827173537242593)
XLA Ops:
  0.6 41.0 %shard_map.139 = (bf16[512,256]{1,0:T(8,128)(2,1)}, f32[1,16]{1,0:T(1,128)}, f32[1,1]{1,0:T(1,128)}) custom-call(f32[512,512]{1,0:T(8,128)} %logits.1, s32[512,512]{1,0:T(8,128)} %target_ref.1, f32[1,16]{1,0:T(1,128)} %bitcast.5, s32[2,16]{1,0:T(2,128)} %bitcast.4, bf16[512,128]{1,0:T(8,128)(2,1)} %constant.16.clone.cf_hbm, ...), custom_call_target="tpu_custom_call" | custom-call | tf_op jit(solution)/shard_map/pallas_call | solution.py:545
  41.6 4.6 %shard_map.140 = (f32[512,512]{1,0:T(8,128)}, f32[1,16]{1,0:T(1,128)}, f32[1,1]{1,0:T(1,128)}) custom-call(bf16[512,256]{1,0:T(8,128)(2,1)} %get-tuple-element.9.column_grad, f32[512,512]{1,0:T(8,128)} %logits.1, bf16[256,512]{1,0:T(8,128)(2,1)} %constant.23.clone.cft, f32[1,16]{1,0:T(1,128)} %get-tuple-element.10.weight_in, f32[1,1]{1,0:T(1,128)} %get-tuple-element.11.loss_in), custom_call_target="tpu_custom_call" | custom-call | tf_op jit(solution)/shard_map/pallas_call | solution.py:587

commit v3 on v2

--- a/solution.py
+++ b/solution.py
@@ -18,6 +18,7 @@
 BOTH = 2 * FREQS
 LANES = 128
 GROUP = 4
+WIDE_GROUP = 8
 MESH = pl.DeviceIdType.MESH
 F32 = jnp.float32
 BF16 = jnp.bfloat16
@@ -295,7 +296,7 @@
             row_fields[pl.ds(start, rows), :] = both[:, i * BOTH : (i + 1) * BOTH]
         return carry
 
-    lax.fori_loop(0, sources // 2, row_step, 0, unroll=4)
+    lax.fori_loop(0, sources // 2, row_step, 0, unroll=8)
 
     target_copy.wait()
     span = GROUP * rows
@@ -315,7 +316,7 @@
             return image
 
         image = lax.fori_loop(
-            0, sources // GROUP, field_step, jnp.zeros((rows, LANES), F32), unroll=4
+            0, sources // GROUP, field_step, jnp.zeros((rows, LANES), F32), unroll=8
         )
         printed = jax.nn.sigmoid(STEEPNESS * (image - THRESHOLD))
         wanted = target_buf[:, q * LANES : (q + 1) * LANES].astype(F32)
@@ -328,8 +329,8 @@
     adjoint_rows = rit_ref[:, pl.ds(my_rows, rows)]
 
     def weigh(group, grads):
-        for i in range(GROUP):
-            s = group * GROUP + i
+        for i in range(WIDE_GROUP):
+            s = group * WIDE_GROUP + i
             doubled_weight = 2.0 * wide[2, pl.ds(s, 1), :]
             total = jnp.zeros((8, LANES), F32)
             for q in range(chunks):
@@ -347,7 +348,7 @@
     def adjoint(group, grads, carry):
         row_grad = dot(grads[...], cit_ref[...]).astype(BF16)
         top, low = carry
-        for pair in range(GROUP // 2):
+        for pair in range(WIDE_GROUP // 2):
             begin = 2 * pair * rows
             block_grad = dot(
                 adjoint_rows,
@@ -356,7 +357,7 @@
                 ),
             )
             for i in range(2):
-                pupil = pupils[group * GROUP + 2 * pair + i]
+                pupil = pupils[group * WIDE_GROUP + 2 * pair + i]
                 one = block_grad[:, i * BOTH : (i + 1) * BOTH]
                 top = top + pupil * one[:FREQS]
                 low = low + pupil * one[FREQS:]
@@ -368,7 +369,7 @@
         weigh(2 * step + 2, even_grads)
         return adjoint(2 * step + 1, odd_grads, carry)
 
-    groups = sources // GROUP
+    groups = sources // WIDE_GROUP
     zero = jnp.zeros((FREQS, BOTH), F32)
     weigh(0, even_grads)
     carry = lax.fori_loop(0, groups // 2 - 1, grad_step, (zero, zero))
@@ -518,13 +519,6 @@
         return carry
 
     lax.fori_loop(1, n_tile, end_stat, 0)
-
-
-def last_kernel(column_grad, logits, cft, weight_in, loss_in, mask_grad, weight_grad, loss):
-    opening = jax.nn.sigmoid(logits[...])
-    mask_grad[...] = dot(column_grad[...], cft[...]) * opening * (1.0 - opening)
-    weight_grad[...] = weight_in[...]
-    loss[...] = loss_in[...]
 
 
 def on_device(n_src, n_tile, mask_logits, target, weights, shifts):
@@ -558,8 +552,8 @@
             pltpu.VMEM((sources * rows, BOTH), BF16),
             pltpu.VMEM((chunks, sources * rows, 2 * LANES), F32),
             pltpu.VMEM((chunks, rows, LANES), F32),
-            pltpu.VMEM((GROUP * rows, 2 * cols), BF16),
-            pltpu.VMEM((GROUP * rows, 2 * cols), BF16),
+            pltpu.VMEM((WIDE_GROUP * rows, 2 * cols), BF16),
+            pltpu.VMEM((WIDE_GROUP * rows, 2 * cols), BF16),
             pltpu.VMEM((sources, 8, LANES), F32),
             pltpu.VMEM((n_src, FREQS + 8, BOTH), F32),
             pltpu.VMEM((3, FREQS, BOTH), F32),
@@ -581,21 +575,8 @@
             collective_id=0, has_side_effects=True, vmem_limit_bytes=56 * 1024 * 1024
         ),
     )(mask_logits, target, weights.reshape(1, local), shifts.T, *tables)
-    steps = 4
-    block = tile_rows // steps
-    whole_small = [pl.BlockSpec(x.shape, lambda i: (0, 0)) for x in small]
-    mask_grad, weight_grad, loss = pl.pallas_call(
-        last_kernel,
-        grid=(steps,),
-        out_shape=(jax.ShapeDtypeStruct((tile_rows, cols), F32),) + small,
-        in_specs=[
-            pl.BlockSpec((block, 2 * BOTH), lambda i: (i, 0)),
-            pl.BlockSpec((block, cols), lambda i: (i, 0)),
-            pl.BlockSpec((2 * BOTH, cols), lambda i: (0, 0)),
-        ]
-        + whole_small,
-        out_specs=tuple([pl.BlockSpec((block, cols), lambda i: (i, 0))] + whole_small),
-    )(column_grad, mask_logits, last_table, weight_grad, loss)
+    opening = jax.nn.sigmoid(mask_logits)
+    mask_grad = dot(column_grad, last_table) * opening * (1.0 - opening)
     return mask_grad, weight_grad.reshape(local), loss.reshape(())
 
 

time: 46.4 us -> 43.5 us (0.938)
  Pallas kernels: 45.6 us -> 38.1 us
  matrix products: 0 us -> 2.33 us
  between operations: 0.64 us -> 2.37 us
  local copies, waits for them, and re-layouts: 0 us -> 0.53 us
    pallas_call x1 -> x0, Pallas kernels: 4.58 us -> none  [on_device(): pl.pallas_call(last_kernel, grid=(steps,), out_shape=(jax.ShapeDtypeStruc...]
    pallas_call x1, Pallas kernels: 41 us -> 38.1 us  [on_device(): pl.pallas_call(functools.partial(kernel, n_src, n_tile), out_shape=(jax.S...]
    dot_general x0 -> x1, matrix products: none -> 2.33 us  [dot(): return jnp.dot(a, b, preferred_element_type=F32)]
    unnamed x0 -> x7, local copies, waits for them, and re-layouts: none -> 0.53 us
where the time goes in v3:
time: 43.5 us; the launch traced here: 43.4 us
  Pallas kernels  38.1 us (88%)
  between operations  2.37 us (5%)
  matrix products  2.33 us (5%)
  local copies, waits for them, and re-layouts  0.53 us (1%)
    pallas_call x1, Pallas kernels, on_device(): pl.pallas_call(functools.partial(kernel, n_src, n_tile), out_shape=(jax.S...  38.1 us
    dot_general x1, matrix products, dot(): return jnp.dot(a, b, preferred_element_type=F32)  2.33 us

profile of v3, /device:TPU:0, one launch (start us, length us, event | category | flops | bytes accessed | tf_op | source)
XLA Modules:
  0.0 43.4 jit_solution(8632835428371379371)
XLA Ops:
  0.6 0.0 copy-start
  0.6 0.0 copy-start.2
  0.7 38.1 %shard_map.139 = (bf16[512,256]{1,0:T(8,128)(2,1)}, f32[1,16]{1,0:T(1,128)}, f32[1,1]{1,0:T(1,128)}) custom-call(f32[512,512]{1,0:T(8,128)} %logits_hbm.1, s32[512,512]{1,0:T(8,128)} %target_ref.1, f32[1,16]{1,0:T(1,128)} %bitcast.7, s32[2,16]{1,0:T(2,128)} %bitcast.6, bf16[512,128]{1,0:T(8,128)(2,1)} %constant.18.clone.cf_hbm, ...), custom_call_target="tpu_custom_call" | custom-call | tf_op jit(solution)/shard_map/pallas_call | solution.py:539
  38.8 0.0 copy-done
  38.8 0.0 copy-done.2
  38.8 0.0 copy-start.1
  38.8 2.3 %fusion = f32[512,512]{1,0:T(8,128)} fusion(bf16[512,256]{1,0:T(8,128)(2,1)} %get-tuple-element.6, bf16[256,512]{1,0:T(8,128)(2,1)S(1)} %copy-done.2, f32[512,512]{1,0:T(8,128)S(1)} %copy-done), kind=kOutput, calls=%fused_computation.1 | convolution fusion | flops 135790592 | bytes 2621440 | tf_op jit(solution)/shard_map/dot_general | solution.py:74
  41.2 0.0 copy-done.1
  41.2 0.5 %copy.17 = f32[16]{0:T(128)} copy(f32[16]{0:T(128)S(1)} %bitcast.8) | data formatting | bytes 128
Async XLA Ops:
  0.6 38.2 %copy-start = (f32[512,512]{1,0:T(8,128)S(1)}, f32[512,512]{1,0:T(8,128)}, u32[]{:S(2)}) copy-start(f32[512,512]{1,0:T(8,128)} %logits_hbm.1) | copy-start | bytes 3145732
  0.6 38.2 %copy-start.2 = (bf16[256,512]{1,0:T(8,128)(2,1)S(1)}, bf16[256,512]{1,0:T(8,128)(2,1)}, u32[]{:S(2)}) copy-start(bf16[256,512]{1,0:T(8,128)(2,1)} %constant.25.clone) | copy-start | bytes 786436
  38.8 2.3 %copy-start.1 = (f32[1,16]{1,0:T(1,128)S(1)}, f32[1,16]{1,0:T(1,128)}, u32[]{:S(2)}) copy-start(f32[1,16]{1,0:T(1,128)} %get-tuple-element.7) | copy-start | bytes 196

commit v4 on v3

--- a/solution.py
+++ b/solution.py
@@ -49,22 +49,22 @@
     real_part = rounded(np.concatenate([cosine_scaled, -sine_scaled], 0))
     imag_part = rounded(np.concatenate([sine_scaled, cosine_scaled], 0))
     chunks = col_count // LANES
-    column_inverse = np.stack(
+    column_inverse = np.concatenate(
         [
             np.concatenate(
                 [part[:, q * LANES : (q + 1) * LANES] for part in (real_part, imag_part)], 1
             )
             for q in range(chunks)
-        ]
-    )
-    column_adjoint = np.concatenate([column_inverse[q].T for q in range(chunks)], 0)
+        ],
+        1,
+    )
     return (
         column_forward,
         row_forward,
         row_inverse,
         np.ascontiguousarray(row_inverse.T),
         column_inverse,
-        np.ascontiguousarray(column_adjoint),
+        np.ascontiguousarray(column_inverse.T),
         np.concatenate([row_forward.T, row_forward.T], 1),
         np.concatenate([column_forward.T, column_forward.T], 0),
     )
@@ -283,42 +283,46 @@
     block_low = -product[FREQS:] - half_sign * turned[:FREQS]
     inverse_rows = ri_ref[...]
 
-    def row_step(pair, carry):
+    def row_step(group, carry):
         blocks = []
-        for i in range(2):
-            pupil = pupils[pair * 2 + i]
+        for i in range(GROUP):
+            pupil = pupils[group * GROUP + i]
             blocks.append(
                 jnp.concatenate([pupil * block_top, pupil * block_low], 0).astype(BF16)
             )
-        both = dot(inverse_rows, jnp.concatenate(blocks, 1)).astype(BF16)
-        for i in range(2):
-            start = pl.multiple_of((pair * 2 + i) * rows, rows)
-            row_fields[pl.ds(start, rows), :] = both[:, i * BOTH : (i + 1) * BOTH]
-        return carry
-
-    lax.fori_loop(0, sources // 2, row_step, 0, unroll=8)
+        together = dot(inverse_rows, jnp.concatenate(blocks, 1)).astype(BF16)
+        for i in range(GROUP):
+            start = pl.multiple_of((group * GROUP + i) * rows, rows)
+            row_fields[pl.ds(start, rows), :] = together[:, i * BOTH : (i + 1) * BOTH]
+        return carry
+
+    lax.fori_loop(0, sources // GROUP, row_step, 0, unroll=4)
+
+    span = GROUP * rows
+    cot[...] = jnp.zeros(cot.shape, F32)
+
+    def field_step(group, carry):
+        place = pl.ds(pl.multiple_of(group * span, span), span)
+        values = dot(row_fields[place, :], ci_ref[...])
+        weight = [wide[2, pl.ds(group * GROUP + i, 1), :] for i in range(GROUP)]
+        for q in range(chunks):
+            real = values[:, 2 * q * LANES : (2 * q + 1) * LANES]
+            imag = values[:, (2 * q + 1) * LANES : (2 * q + 2) * LANES]
+            fields[q, place, :LANES] = real
+            fields[q, place, LANES:] = imag
+            power = real * real + imag * imag
+            image = cot[q]
+            for i in range(GROUP):
+                image = image + weight[i] * power[i * rows : (i + 1) * rows]
+            cot[q] = image
+        return carry
+
+    lax.fori_loop(0, sources // GROUP, field_step, 0, unroll=4)
 
     target_copy.wait()
-    span = GROUP * rows
     error_sum = jnp.zeros((1, LANES), F32)
     for q in range(chunks):
-        inverse_chunk = ci_ref[q]
-
-        def field_step(group, image, q=q, inverse_chunk=inverse_chunk):
-            place = pl.ds(pl.multiple_of(group * span, span), span)
-            values = dot(row_fields[place, :], inverse_chunk)
-            fields[q, place, :] = values
-            real, imag = values[:, :LANES], values[:, LANES:]
-            power = real * real + imag * imag
-            for i in range(GROUP):
-                weight = wide[2, pl.ds(group * GROUP + i, 1), :]
-                image = image + weight * power[i * rows : (i + 1) * rows]
-            return image
-
-        image = lax.fori_loop(
-            0, sources // GROUP, field_step, jnp.zeros((rows, LANES), F32), unroll=8
-        )
-        printed = jax.nn.sigmoid(STEEPNESS * (image - THRESHOLD))
+        printed = jax.nn.sigmoid(STEEPNESS * (cot[q] - THRESHOLD))
         wanted = target_buf[:, q * LANES : (q + 1) * LANES].astype(F32)
         error = printed - wanted
         cot[q] = 2.0 * STEEPNESS * error * printed * (1.0 - printed)
@@ -346,18 +350,15 @@
             terms[s] = total
 
     def adjoint(group, grads, carry):
-        row_grad = dot(grads[...], cit_ref[...]).astype(BF16)
         top, low = carry
-        for pair in range(WIDE_GROUP // 2):
-            begin = 2 * pair * rows
+        for part in range(WIDE_GROUP // GROUP):
+            row_grad = dot(grads[part * span : (part + 1) * span, :], cit_ref[...]).astype(BF16)
             block_grad = dot(
                 adjoint_rows,
-                jnp.concatenate(
-                    [row_grad[begin : begin + rows], row_grad[begin + rows : begin + 2 * rows]], 1
-                ),
+                jnp.concatenate([row_grad[i * rows : (i + 1) * rows] for i in range(GROUP)], 1),
             )
-            for i in range(2):
-                pupil = pupils[group * WIDE_GROUP + 2 * pair + i]
+            for i in range(GROUP):
+                pupil = pupils[group * WIDE_GROUP + part * GROUP + i]
                 one = block_grad[:, i * BOTH : (i + 1) * BOTH]
                 top = top + pupil * one[:FREQS]
                 low = low + pupil * one[FREQS:]

time: 43.5 us -> 42.1 us (0.968)
  Pallas kernels: 38.1 us -> 36.7 us
    pallas_call x1, Pallas kernels: 38.1 us -> 36.7 us  [on_device(): pl.pallas_call(functools.partial(kernel, n_src, n_tile), out_shape=(jax.S...]
where the time goes in v4:
time: 42.1 us; the launch traced here: 41.9 us
  Pallas kernels  36.7 us (87%)
  between operations  2.37 us (6%)
  matrix products  2.34 us (6%)
  local copies, waits for them, and re-layouts  0.53 us (1%)
    pallas_call x1, Pallas kernels, on_device(): pl.pallas_call(functools.partial(kernel, n_src, n_tile), out_shape=(jax.S...  36.7 us
    dot_general x1, matrix products, dot(): return jnp.dot(a, b, preferred_element_type=F32)  2.34 us

profile of v4, /device:TPU:0, one launch (start us, length us, event | category | flops | bytes accessed | tf_op | source)
XLA Modules:
  0.0 41.9 jit_solution(9994305114492977749)
XLA Ops:
  0.6 0.0 copy-start
  0.6 0.0 copy-start.2
  0.7 36.7 %shard_map.139 = (bf16[512,256]{1,0:T(8,128)(2,1)}, f32[1,16]{1,0:T(1,128)}, f32[1,1]{1,0:T(1,128)}) custom-call(f32[512,512]{1,0:T(8,128)} %logits_hbm.1, s32[512,512]{1,0:T(8,128)} %target_ref.1, f32[1,16]{1,0:T(1,128)} %bitcast.7, s32[2,16]{1,0:T(2,128)} %bitcast.6, bf16[512,128]{1,0:T(8,128)(2,1)} %constant.18.clone.cf_hbm, ...), custom_call_target="tpu_custom_call" | custom-call | tf_op jit(solution)/shard_map/pallas_call | solution.py:540
  37.3 0.0 copy-done
  37.3 0.0 copy-done.2
  37.3 0.0 copy-start.1
  37.4 2.3 %fusion = f32[512,512]{1,0:T(8,128)} fusion(bf16[512,256]{1,0:T(8,128)(2,1)} %get-tuple-element.6, bf16[256,512]{1,0:T(8,128)(2,1)S(1)} %copy-done.2, f32[512,512]{1,0:T(8,128)S(1)} %copy-done), kind=kOutput, calls=%fused_computation.1 | convolution fusion | flops 135790592 | bytes 2621440 | tf_op jit(solution)/shard_map/dot_general | solution.py:74
  39.7 0.0 copy-done.1
  39.7 0.5 %copy.17 = f32[16]{0:T(128)} copy(f32[16]{0:T(128)S(1)} %bitcast.8) | data formatting | bytes 128
Async XLA Ops:
  0.6 36.7 %copy-start = (f32[512,512]{1,0:T(8,128)S(1)}, f32[512,512]{1,0:T(8,128)}, u32[]{:S(2)}) copy-start(f32[512,512]{1,0:T(8,128)} %logits_hbm.1) | copy-start | bytes 3145732
  0.6 36.7 %copy-start.2 = (bf16[256,512]{1,0:T(8,128)(2,1)S(1)}, bf16[256,512]{1,0:T(8,128)(2,1)}, u32[]{:S(2)}) copy-start(bf16[256,512]{1,0:T(8,128)(2,1)} %constant.25.clone) | copy-start | bytes 786436
  37.3 2.4 %copy-start.1 = (f32[1,16]{1,0:T(1,128)S(1)}, f32[1,16]{1,0:T(1,128)}, u32[]{:S(2)}) copy-start(f32[1,16]{1,0:T(1,128)} %get-tuple-element.7) | copy-start | bytes 196

commit v5 on v4

--- a/solution.py
+++ b/solution.py
@@ -19,6 +19,7 @@
 LANES = 128
 GROUP = 4
 WIDE_GROUP = 8
+PIECE = 32
 MESH = pl.DeviceIdType.MESH
 F32 = jnp.float32
 BF16 = jnp.bfloat16
@@ -116,6 +117,7 @@
     even_grads,
     odd_grads,
     terms,
+    spectrum_sum,
     shares,
     beside,
     stats,
@@ -304,17 +306,18 @@
     def field_step(group, carry):
         place = pl.ds(pl.multiple_of(group * span, span), span)
         values = dot(row_fields[place, :], ci_ref[...])
+        for q in range(chunks):
+            fields[q, place, :] = values[:, 2 * q * LANES : 2 * (q + 1) * LANES]
         weight = [wide[2, pl.ds(group * GROUP + i, 1), :] for i in range(GROUP)]
         for q in range(chunks):
-            real = values[:, 2 * q * LANES : (2 * q + 1) * LANES]
-            imag = values[:, (2 * q + 1) * LANES : (2 * q + 2) * LANES]
-            fields[q, place, :LANES] = real
-            fields[q, place, LANES:] = imag
-            power = real * real + imag * imag
-            image = cot[q]
-            for i in range(GROUP):
-                image = image + weight[i] * power[i * rows : (i + 1) * rows]
-            cot[q] = image
+            for r in range(0, rows, PIECE):
+                image = cot[q, r : r + PIECE, :]
+                for i in range(GROUP):
+                    start = pl.multiple_of((group * GROUP + i) * rows + r, PIECE)
+                    part = fields[q, pl.ds(start, PIECE), :]
+                    real, imag = part[:, :LANES], part[:, LANES:]
+                    image = image + weight[i] * (real * real + imag * imag)
+                cot[q, r : r + PIECE, :] = image
         return carry
 
     lax.fori_loop(0, sources // GROUP, field_step, 0, unroll=4)
@@ -338,45 +341,49 @@
             doubled_weight = 2.0 * wide[2, pl.ds(s, 1), :]
             total = jnp.zeros((8, LANES), F32)
             for q in range(chunks):
-                part = fields[q, pl.ds(pl.multiple_of(s * rows, rows), rows), :]
-                real, imag = part[:, :LANES], part[:, LANES:]
-                scaling = doubled_weight * cot[q]
-                real_grad, imag_grad = scaling * real, scaling * imag
-                term = real_grad * real + imag_grad * imag
-                total = total + jnp.sum(term.reshape(rows // 8, 8, LANES), axis=0)
-                at = slice(i * rows, (i + 1) * rows)
-                grads[at, 2 * q * LANES : (2 * q + 1) * LANES] = real_grad.astype(BF16)
-                grads[at, (2 * q + 1) * LANES : (2 * q + 2) * LANES] = imag_grad.astype(BF16)
+                for r in range(0, rows, PIECE):
+                    start = pl.multiple_of(s * rows + r, PIECE)
+                    part = fields[q, pl.ds(start, PIECE), :]
+                    real, imag = part[:, :LANES], part[:, LANES:]
+                    scaling = doubled_weight * cot[q, r : r + PIECE, :]
+                    real_grad, imag_grad = scaling * real, scaling * imag
+                    term = real_grad * real + imag_grad * imag
+                    total = total + jnp.sum(term.reshape(PIECE // 8, 8, LANES), axis=0)
+                    at = slice(i * rows + r, i * rows + r + PIECE)
+                    grads[at, 2 * q * LANES : (2 * q + 1) * LANES] = real_grad.astype(BF16)
+                    grads[at, (2 * q + 1) * LANES : (2 * q + 2) * LANES] = imag_grad.astype(BF16)
             terms[s] = total
 
-    def adjoint(group, grads, carry):
-        top, low = carry
+    def adjoint(group, grads):
         for part in range(WIDE_GROUP // GROUP):
             row_grad = dot(grads[part * span : (part + 1) * span, :], cit_ref[...]).astype(BF16)
             block_grad = dot(
                 adjoint_rows,
                 jnp.concatenate([row_grad[i * rows : (i + 1) * rows] for i in range(GROUP)], 1),
             )
-            for i in range(GROUP):
-                pupil = pupils[group * WIDE_GROUP + part * GROUP + i]
-                one = block_grad[:, i * BOTH : (i + 1) * BOTH]
-                top = top + pupil * one[:FREQS]
-                low = low + pupil * one[FREQS:]
-        return top, low
+            for half in range(2):
+                at = slice(half * FREQS, (half + 1) * FREQS)
+                added = spectrum_sum[at, :]
+                for i in range(GROUP):
+                    pupil = pupils[group * WIDE_GROUP + part * GROUP + i]
+                    added = added + pupil * block_grad[at, i * BOTH : (i + 1) * BOTH]
+                spectrum_sum[at, :] = added
 
     def grad_step(step, carry):
         weigh(2 * step + 1, odd_grads)
-        carry = adjoint(2 * step, even_grads, carry)
+        adjoint(2 * step, even_grads)
         weigh(2 * step + 2, even_grads)
-        return adjoint(2 * step + 1, odd_grads, carry)
+        adjoint(2 * step + 1, odd_grads)
+        return carry
 
     groups = sources // WIDE_GROUP
-    zero = jnp.zeros((FREQS, BOTH), F32)
+    spectrum_sum[...] = jnp.zeros((BOTH, BOTH), F32)
     weigh(0, even_grads)
-    carry = lax.fori_loop(0, groups // 2 - 1, grad_step, (zero, zero))
+    lax.fori_loop(0, groups // 2 - 1, grad_step, 0)
     weigh(groups - 1, odd_grads)
-    carry = adjoint(groups - 2, even_grads, carry)
-    top, low = adjoint(groups - 1, odd_grads, carry)
+    adjoint(groups - 2, even_grads)
+    adjoint(groups - 1, odd_grads)
+    top, low = spectrum_sum[:FREQS, :], spectrum_sum[FREQS:, :]
 
     shares[src, 0:FREQS, :] = top + half_sign * pltpu.roll(low, FREQS, 1)
     source_column = jnp.sum(jnp.sum(terms[...], axis=1), axis=1, keepdims=True) / (
@@ -556,6 +563,7 @@
             pltpu.VMEM((WIDE_GROUP * rows, 2 * cols), BF16),
             pltpu.VMEM((WIDE_GROUP * rows, 2 * cols), BF16),
             pltpu.VMEM((sources, 8, LANES), F32),
+            pltpu.VMEM((BOTH, BOTH), F32),
             pltpu.VMEM((n_src, FREQS + 8, BOTH), F32),
             pltpu.VMEM((3, FREQS, BOTH), F32),
             pltpu.VMEM((n_tile, 8, LANES), F32),

time: 42.1 us -> 44.8 us (1.064)
  Pallas kernels: 36.7 us -> 39.4 us
    pallas_call x1, Pallas kernels: 36.7 us -> 39.4 us  [on_device(): pl.pallas_call(functools.partial(kernel, n_src, n_tile), out_shape=(jax.S...]
where the time goes in v5:
time: 44.8 us; the launch traced here: 44.6 us
  Pallas kernels  39.4 us (88%)
  between operations  2.37 us (5%)
  matrix products  2.34 us (5%)
  local copies, waits for them, and re-layouts  0.53 us (1%)
    pallas_call x1, Pallas kernels, on_device(): pl.pallas_call(functools.partial(kernel, n_src, n_tile), out_shape=(jax.S...  39.4 us
    dot_general x1, matrix products, dot(): return jnp.dot(a, b, preferred_element_type=F32)  2.34 us

profile of v5, /device:TPU:0, one launch (start us, length us, event | category | flops | bytes accessed | tf_op | source)
XLA Modules:
  0.0 44.6 jit_solution(4745747825359872886)
XLA Ops:
  0.6 0.0 copy-start
  0.6 0.0 copy-start.2
  0.7 39.4 %shard_map.139 = (bf16[512,256]{1,0:T(8,128)(2,1)}, f32[1,16]{1,0:T(1,128)}, f32[1,1]{1,0:T(1,128)}) custom-call(f32[512,512]{1,0:T(8,128)} %logits_hbm.1, s32[512,512]{1,0:T(8,128)} %target_ref.1, f32[1,16]{1,0:T(1,128)} %bitcast.7, s32[2,16]{1,0:T(2,128)} %bitcast.6, bf16[512,128]{1,0:T(8,128)(2,1)} %constant.18.clone.cf_hbm, ...), custom_call_target="tpu_custom_call" | custom-call | tf_op jit(solution)/shard_map/pallas_call | solution.py:547
  40.0 0.0 copy-done
  40.0 0.0 copy-done.2
  40.0 0.0 copy-start.1
  40.1 2.3 %fusion = f32[512,512]{1,0:T(8,128)} fusion(bf16[512,256]{1,0:T(8,128)(2,1)} %get-tuple-element.6, bf16[256,512]{1,0:T(8,128)(2,1)S(1)} %copy-done.2, f32[512,512]{1,0:T(8,128)S(1)} %copy-done), kind=kOutput, calls=%fused_computation.1 | convolution fusion | flops 135790592 | bytes 2621440 | tf_op jit(solution)/shard_map/dot_general | solution.py:75
  42.4 0.0 copy-done.1
  42.4 0.5 %copy.17 = f32[16]{0:T(128)} copy(f32[16]{0:T(128)S(1)} %bitcast.8) | data formatting | bytes 128
Async XLA Ops:
  0.6 39.4 %copy-start = (f32[512,512]{1,0:T(8,128)S(1)}, f32[512,512]{1,0:T(8,128)}, u32[]{:S(2)}) copy-start(f32[512,512]{1,0:T(8,128)} %logits_hbm.1) | copy-start | bytes 3145732
  0.6 39.4 %copy-start.2 = (bf16[256,512]{1,0:T(8,128)(2,1)S(1)}, bf16[256,512]{1,0:T(8,128)(2,1)}, u32[]{:S(2)}) copy-start(bf16[256,512]{1,0:T(8,128)(2,1)} %constant.25.clone) | copy-start | bytes 786436
  40.0 2.3 %copy-start.1 = (f32[1,16]{1,0:T(1,128)S(1)}, f32[1,16]{1,0:T(1,128)}, u32[]{:S(2)}) copy-start(f32[1,16]{1,0:T(1,128)} %get-tuple-element.7) | copy-start | bytes 196

commit v6 on v4

--- a/solution.py
+++ b/solution.py
@@ -296,7 +296,7 @@
             row_fields[pl.ds(start, rows), :] = together[:, i * BOTH : (i + 1) * BOTH]
         return carry
 
-    lax.fori_loop(0, sources // GROUP, row_step, 0, unroll=4)
+    lax.fori_loop(0, sources // GROUP, row_step, 0, unroll=16)
 
     span = GROUP * rows
     cot[...] = jnp.zeros(cot.shape, F32)
@@ -317,7 +317,7 @@
             cot[q] = image
         return carry
 
-    lax.fori_loop(0, sources // GROUP, field_step, 0, unroll=4)
+    lax.fori_loop(0, sources // GROUP, field_step, 0, unroll=8)
 
     target_copy.wait()
     error_sum = jnp.zeros((1, LANES), F32)

time: 42.1 us -> 41.5 us (0.986)
  Pallas kernels: 36.7 us -> 36 us
    pallas_call x1, Pallas kernels: 36.7 us -> 36 us  [on_device(): pl.pallas_call(functools.partial(kernel, n_src, n_tile), out_shape=(jax.S...]
where the time goes in v6:
time: 41.5 us; the launch traced here: 41.3 us
  Pallas kernels  36 us (87%)
  between operations  2.37 us (6%)
  matrix products  2.33 us (6%)
  local copies, waits for them, and re-layouts  0.53 us (1%)
    pallas_call x1, Pallas kernels, on_device(): pl.pallas_call(functools.partial(kernel, n_src, n_tile), out_shape=(jax.S...  36 us
    dot_general x1, matrix products, dot(): return jnp.dot(a, b, preferred_element_type=F32)  2.33 us

profile of v6, /device:TPU:0, one launch (start us, length us, event | category | flops | bytes accessed | tf_op | source)
XLA Modules:
  0.0 41.3 jit_solution(6558464483649183547)
XLA Ops:
  0.6 0.0 copy-start
  0.6 0.0 copy-start.2
  0.7 36.0 %shard_map.139 = (bf16[512,256]{1,0:T(8,128)(2,1)}, f32[1,16]{1,0:T(1,128)}, f32[1,1]{1,0:T(1,128)}) custom-call(f32[512,512]{1,0:T(8,128)} %logits_hbm.1, s32[512,512]{1,0:T(8,128)} %target_ref.1, f32[1,16]{1,0:T(1,128)} %bitcast.7, s32[2,16]{1,0:T(2,128)} %bitcast.6, bf16[512,128]{1,0:T(8,128)(2,1)} %constant.18.clone.cf_hbm, ...), custom_call_target="tpu_custom_call" | custom-call | tf_op jit(solution)/shard_map/pallas_call | solution.py:540
  36.7 0.0 copy-done
  36.7 0.0 copy-done.2
  36.7 0.0 copy-start.1
  36.7 2.3 %fusion = f32[512,512]{1,0:T(8,128)} fusion(bf16[512,256]{1,0:T(8,128)(2,1)} %get-tuple-element.6, bf16[256,512]{1,0:T(8,128)(2,1)S(1)} %copy-done.2, f32[512,512]{1,0:T(8,128)S(1)} %copy-done), kind=kOutput, calls=%fused_computation.1 | convolution fusion | flops 135790592 | bytes 2621440 | tf_op jit(solution)/shard_map/dot_general | solution.py:74
  39.1 0.0 copy-done.1
  39.1 0.5 %copy.17 = f32[16]{0:T(128)} copy(f32[16]{0:T(128)S(1)} %bitcast.8) | data formatting | bytes 128
Async XLA Ops:
  0.6 36.1 %copy-start = (f32[512,512]{1,0:T(8,128)S(1)}, f32[512,512]{1,0:T(8,128)}, u32[]{:S(2)}) copy-start(f32[512,512]{1,0:T(8,128)} %logits_hbm.1) | copy-start | bytes 3145732
  0.6 36.1 %copy-start.2 = (bf16[256,512]{1,0:T(8,128)(2,1)S(1)}, bf16[256,512]{1,0:T(8,128)(2,1)}, u32[]{:S(2)}) copy-start(bf16[256,512]{1,0:T(8,128)(2,1)} %constant.25.clone) | copy-start | bytes 786436
  36.7 2.3 %copy-start.1 = (f32[1,16]{1,0:T(1,128)S(1)}, f32[1,16]{1,0:T(1,128)}, u32[]{:S(2)}) copy-start(f32[1,16]{1,0:T(1,128)} %get-tuple-element.7) | copy-start | bytes 196
